TPU v7x, 512 devices: a whole 4x8x8 slice. The times are simulated.
512 devices in a mesh: dp: 32 (over x, z), tensor: 16 (over y, core).
Axes of the slice: x: 4, y: 8, z: 8, core: 2. Of those that a mesh axis runs over, the one named last changes fastest.
Arguments:
- hidden: bfloat16 [8192, 18432], P('dp', 'tensor'), may hold values from -1.5 to 1.5
- grad_out: bfloat16 [8192, 2304], P('dp'), may hold values from -1.5 to 1.5
- q_init: bfloat16 [2304, 128], P('tensor'), may hold values from -6 to 6
- error: bfloat16 [32, 18432, 1152], P('dp', 'tensor'), may hold values from -6 to 6
Outputs:
- p_hat: bfloat16 [18432, 128], P('tensor')
- q_new: bfloat16 [2304, 128], P('tensor')
All inputs are finite; a program needn't handle non-finite values.
Results may differ from a plain program's by a relative error of at most 0.0051.
Values may be sent and summed in bfloat16 or wider, within the bound.
No kernel may reach another device: no remote copies, remote signals or barrier semaphores. Data moves between devices by JAX's collectives and lax.ppermute only.
A program may use at most 64 MiB of HBM per device.

v0:
```python
import jax
import jax.numpy as jnp
from jax import lax
from jax.sharding import PartitionSpec as P


def swapped(value, axis, bit):
    mask = 2**bit
    pairs = [(source, source ^ mask) for source in range(lax.axis_size(axis))]
    return lax.ppermute(value, axis, pairs)


def orthonormal(rows, gram):
    low = jnp.linalg.cholesky(gram)
    return lax.linalg.triangular_solve(low, rows, left_side=False, lower=True, transpose_a=True)


def shards(hidden, grad_out, q_init, error):
    replicas = lax.axis_size("dp") // 2
    side = lax.axis_index("dp") % 2
    width = grad_out.shape[1]
    half = width // 2
    own_cols = lax.dynamic_slice_in_dim(grad_out, side * half, half, 1)
    their_cols = lax.dynamic_slice_in_dim(grad_out, (1 - side) * half, half, 1)
    partner_hid = swapped(hidden, "dp", 0)
    partner_out = swapped(their_cols, "dp", 0)
    grad_half = lax.dot_general(
        hidden, own_cols, (((0,), (0,)), ((), ())), preferred_element_type=jnp.float32
    )
    grad_half = grad_half + lax.dot_general(
        partner_hid, partner_out, (((0,), (0,)), ((), ())), preferred_element_type=jnp.float32
    )
    corrected = (grad_half + error[0].astype(jnp.float32)).astype(jnp.bfloat16)
    q_whole = lax.all_gather(q_init, "tensor", axis=0, tiled=True)
    q_mine = lax.dynamic_slice_in_dim(q_whole, side * half, half, 0)
    term = jnp.dot(corrected, q_mine, preferred_element_type=jnp.float32)
    p_sum = lax.psum(term, "dp") / replicas
    gram = lax.psum(jnp.dot(p_sum.T, p_sum, precision=lax.Precision.HIGHEST), "tensor")
    p_round = orthonormal(p_sum, gram).astype(jnp.bfloat16)
    q_term = lax.dot_general(
        corrected, p_round, (((0,), (0,)), ((), ())), preferred_element_type=jnp.float32
    )
    first = (side == 0).astype(jnp.float32)
    block_rows = width // lax.axis_size("tensor")
    padded = jnp.concatenate([q_term * first, q_term * (1.0 - first)], axis=0)
    total = lax.psum(padded, ("dp", "tensor")) / replicas
    q_sum = lax.dynamic_slice_in_dim(total, lax.axis_index("tensor") * block_rows, block_rows, 0)
    q_out = q_sum.astype(jnp.bfloat16)
    return (p_round, q_out)


def solution(mesh):
    in_specs = (P("dp", "tensor"), P("dp", None), P("tensor", None), P("dp", "tensor", None))
    out_specs = (P("tensor", None), P("tensor", None))
    return jax.shard_map(shards, mesh=mesh, in_specs=in_specs, out_specs=out_specs, check_vma=False)
```

profile of v0, /device:TPU:1, one launch (start us, length us, event | category | flops | bytes accessed | tf_op | source)
XLA Modules:
  0.0 622.6 jit_solution(8654489169494358216)
XLA Ops:
  7.2 1.2 copy-done
  8.5 4.8 collective-permute-start
  13.3 1.9 collective-permute-start.1
  15.3 5.3 copy.6
  20.6 22.1 %all_gather.3 = bf16[2304,128]{1,0:T(8,128)(2,1)S(1)} all-gather(bf16[144,128]{1,0:T(8,128)(2,1)} %param.6), channel_id=1, replica_groups=mesh['dp'=32,'tensor'=16] {'tensor'}, dimensions={0}, use_global_device_ids=true | all-gather | bytes 626688 | tf_op jit(solution)/shard_map/all_gather | solution.py:34
  42.6 1.0 fusion.3
  43.7 0.7 copy-done.2
  44.4 1.0 fusion.2
  45.4 1.5 copy-done.1
  46.9 1.7 fusion.10
  48.7 154.0 %all-reduce.4.cloned.1.call-done = f32[1152,128]{1,0:T(8,128)} async-done(((f32[1152,128]{1,0:T(8,128)}), f32[1152,128]{1,0:T(8,128)}) %all-reduce.4.cloned.1.call-update) | async-done | bytes 589840 | tf_op jit(solution)/shard_map/psum | solution.py:37
  202.7 3.0 fusion.6
  205.9 106.4 %all-reduce.6.cloned.1.call-done = f32[128,128]{0,1:T(8,128)} async-done(((f32[128,128]{0,1:T(8,128)}), f32[128,128]{0,1:T(8,128)}) %all-reduce.6.cloned.1.call-update) | async-done | bytes 65552 | tf_op jit(solution)/shard_map/psum | solution.py:38
  312.3 0.9 copy.8
  313.2 0.9 fusion.15
  314.1 11.7 %cholesky.16 = f32[128,128]{1,0:T(8,128)S(1)} custom-call(f32[128,128]{1,0:T(8,128)S(1)} %fusion.15), custom_call_target="Cholesky" | custom-call | tf_op jit(solution)/shard_map/jit(cholesky)/cholesky | solution.py:14
  325.8 0.6 compare_reduce_fusion
  326.5 0.7 fusion.13
  327.2 9.8 %custom-call.6 = f32[1,128,128]{1,2,0:T(8,128)S(1)} custom-call(f32[1,128,128]{2,1,0:T(8,128)S(1)} %fusion.13), custom_call_target="InvertDiagBlocksLowerTriangular" | custom-call | tf_op jit(solution)/shard_map/triangular_solve | solution.py:15
  337.0 1.7 convolution_convert_fusion
  338.7 2.7 broadcast_multiply_fusion.1
  341.4 1.1 pad_maximum_fusion
  342.6 272.0 %all-reduce.8.cloned.1.call-done = f32[2304,128]{1,0:T(8,128)} async-done(((f32[2304,128]{1,0:T(8,128)}), f32[2304,128]{1,0:T(8,128)}) %all-reduce.8.cloned.1.call-update) | async-done | bytes 1179664 | tf_op jit(solution)/shard_map/psum | solution.py:46
  614.6 1.5 fusion.12
  (17 shorter events, 0.5 us)
Async XLA Ops:
  7.2 1.3 copy-start
  7.2 195.5 %all-reduce.4.cloned.1.call-start = ((), (), s32[]{:S(2)}) async-start(), calls=%async_computation | async-start | bytes 1179648 | tf_op jit(solution)/shard_map/psum | solution.py:37
  8.5 35.1 %collective-permute-start = (bf16[256,1152]{1,0:T(8,128)(2,1)S(1)}, bf16[256,1152]{1,0:T(8,128)(2,1)S(1)}, u32[]{:S(2)}, u32[]{:S(2)}) collective-permute-start(bf16[256,1152]{1,0:T(8,128)(2,1)S(1)} %constant_dynamic-slice_fusion), channel_id=1, source_target_pairs={{0,16},{16,0},{32,48},{48,32},{64,80},{80,64},{96,112},{112,96},{1... | collective-permute-start | bytes 1769480 | tf_op jit(solution)/shard_map/ppermute | solution.py:10
  13.3 30.3 %collective-permute-start.1 = (bf16[256,1152]{1,0:T(8,128)(2,1)}, bf16[256,1152]{1,0:T(8,128)(2,1)S(1)}, u32[]{:S(2)}, u32[]{:S(2)}) collective-permute-start(bf16[256,1152]{1,0:T(8,128)(2,1)} %param.4), channel_id=1, source_target_pairs={{0,16},{16,0},{32,48},{48,32},{64,80},{80,64},{96,112},{112,96},{1... | collective-permute-start | bytes 1769480 | tf_op jit(solution)/shard_map/ppermute | solution.py:10
  15.3 27.4 %copy-start.4 = (bf16[256,1152]{1,0:T(8,128)(2,1)S(1)}, bf16[256,1152]{1,0:T(8,128)(2,1)}, u32[]{:S(2)}) copy-start(bf16[256,1152]{1,0:T(8,128)(2,1)} %param.4) | copy-start | bytes 1769476
  42.6 1.8 copy-start.2
  45.4 1.5 copy-start.1
  48.7 263.7 %all-reduce.6.cloned.1.call-start = ((), (), s32[]{:S(2)}) async-start(), calls=%async_computation.1 | async-start | bytes 131072 | tf_op jit(solution)/shard_map/psum | solution.py:38
  205.7 408.9 %all-reduce.8.cloned.1.call-start = ((), (), s32[]{:S(2)}) async-start(), calls=%async_computation.2 | async-start | bytes 2359296 | tf_op jit(solution)/shard_map/psum | solution.py:46
  338.7 2.7 copy-start.3
Sparse Core Ops, SparseCore 0:
  48.8 153.8 all-reduce.3
  205.8 106.4 all-reduce.5
  342.7 271.8 all-reduce.7
where the time goes:
time: 623 us
  waiting for transfers between devices  532 us (85%)
  other arithmetic  26.3 us (4%)
  blocking collectives  22.1 us (4%)
  between operations  13.9 us (2%)
  matrix products  11.1 us (2%)
  local copies, waits for them, and re-layouts  9.71 us (2%)
  starting transfers between devices  7.05 us (1%)
    psum x1, waiting for transfers between devices, shards(): total = lax.psum(padded, ('dp', 'tensor')) / replicas  272 us
    psum x1, waiting for transfers between devices, shards(): p_sum = lax.psum(term, 'dp') / replicas  154 us
    psum x1, waiting for transfers between devices, shards(): lax.psum(jnp.dot(p_sum.T, p_sum, precision=lax.Precision.HIGHEST), 'tensor')  106 us
    all_gather x1, blocking collectives, shards(): q_whole = lax.all_gather(q_init, 'tensor', axis=0, tiled=True)  22.1 us
  transfers between devices with their start and end apart: 5, of which 3 were waited for; matrix products, arithmetic and copies ran while one was open for 1% of the time, Pallas kernels for 0%

commit v1 on v0

v1 whole, which is shorter than its diff:
```python
import jax
import jax.numpy as jnp
from jax import lax
from jax.sharding import PartitionSpec as P

F32 = jnp.float32
BF16 = jnp.bfloat16


def swap_blocks(blocks, axis):
    return lax.all_to_all(blocks, axis, 0, 0, tiled=True)


def spread(block, axis):
    return swap_blocks(jnp.broadcast_to(block, (lax.axis_size(axis),) + block.shape), axis)


def dot_rows(a, b):
    return lax.dot_general(a, b, (((0,), (0,)), ((), ())), preferred_element_type=F32)


def shards(hidden, grad_out, q_init, error):
    n_dp, n_tensor = lax.axis_size("dp"), lax.axis_size("tensor")
    replicas = n_dp // 2
    place = lax.axis_index("dp")
    side = place % 2
    width = grad_out.shape[1]
    half = width // 2
    rows, rank = hidden.shape[1], q_init.shape[1]
    err = error[0]

    q_whole = lax.all_gather(q_init, "tensor", axis=0, tiled=True)
    q_mine = lax.dynamic_slice_in_dim(q_whole, side * half, half, 0)
    mixed = jnp.dot(grad_out, q_whole, preferred_element_type=F32).astype(BF16)
    term = dot_rows(hidden, mixed) + jnp.dot(err, q_mine, preferred_element_type=F32)

    chunk = -(-rows // (n_dp * 8)) * 8
    padded = jnp.pad(term, ((0, chunk * n_dp - rows), (0, 0))).reshape(n_dp, chunk, rank)
    p_chunk = jnp.sum(swap_blocks(padded, "dp"), axis=0) / replicas
    p_sum = spread(p_chunk, "dp").reshape(n_dp * chunk, rank)[:rows]

    p_low = p_sum.astype(BF16)
    gram_part = jnp.dot(p_sum.T, p_sum, precision=lax.Precision.HIGHEST)
    hid_p = jnp.dot(hidden, p_low, preferred_element_type=F32).astype(BF16)
    from_err = dot_rows(err, p_low)
    s_part = dot_rows(grad_out, hid_p)
    zero = jnp.zeros_like(from_err)
    s_part = s_part + jnp.where(
        side == 0,
        jnp.concatenate([from_err, zero], axis=0),
        jnp.concatenate([zero, from_err], axis=0),
    )

    block = width // n_tensor
    gram_rows = rank // replicas
    gram_mine = lax.dynamic_slice_in_dim(gram_part, (place // 2) * gram_rows, gram_rows, 0)
    packet = jnp.concatenate(
        [
            s_part.reshape(n_tensor, block, rank),
            jnp.broadcast_to(gram_mine, (n_tensor, gram_rows, rank)),
        ],
        axis=1,
    )
    packet = jnp.sum(swap_blocks(packet, "tensor"), axis=0)
    packets = spread(packet, "dp")
    s_sum = jnp.sum(packets[:, :block], axis=0) / replicas
    gram = packets[::2, block:].reshape(rank, rank)

    low = jnp.linalg.cholesky(gram)
    both = lax.linalg.triangular_solve(
        low, jnp.concatenate([p_sum, s_sum], axis=0), left_side=False, lower=True, transpose_a=True
    )
    both = both.astype(BF16)
    return both[:rows], both[rows:]


def solution(mesh):
    in_specs = (P("dp", "tensor"), P("dp", None), P("tensor", None), P("dp", "tensor", None))
    out_specs = (P("tensor", None), P("tensor", None))
    return jax.shard_map(shards, mesh=mesh, in_specs=in_specs, out_specs=out_specs, check_vma=False)
```

time: 623 us -> 233 us (0.37)
  waiting for transfers between devices: 532 us -> 75.2 us
  blocking collectives: 22.1 us -> 92.3 us
  between operations: 13.9 us -> 0.79 us
    psum x3 -> x0, waiting for transfers between devices: 532 us -> none  [the longest x1 272 us: shards(): total = lax.psum(padded, ('dp', 'tensor')) / replicas]
    all_to_all x0 -> x2, waiting for transfers between devices: none -> 75.2 us  [swap_blocks(): return lax.all_to_all(blocks, axis, 0, 0, tiled=True)]
    all_to_all x0 -> x2, blocking collectives: none -> 69.2 us  [swap_blocks(): return lax.all_to_all(blocks, axis, 0, 0, tiled=True)]
    all_to_all x0 -> x2, starting transfers between devices: none -> 13.2 us  [swap_blocks(): return lax.all_to_all(blocks, axis, 0, 0, tiled=True)]
    unnamed x11 -> x5, local copies, waits for them, and re-layouts: 8.74 us -> 1.3 us
    ppermute x2 -> x0, starting transfers between devices: 6.75 us -> none  [swapped(): return lax.ppermute(value, axis, pairs)]
  transfers between devices with their start and end apart: 5 -> 2, of which waited for: 3 -> 2; matrix products, arithmetic and copies ran while one was open for 1% -> 0% of each run, Pallas kernels for 0% -> 0%
where the time goes in v1:
time: 233 us; the launch traced here: 232 us
  blocking collectives  92.3 us (40%)
  waiting for transfers between devices  75.2 us (32%)
  other arithmetic  28.4 us (12%)
  starting transfers between devices  13.2 us (6%)
  matrix products  12.7 us (5%)
  local copies, waits for them, and re-layouts  9.69 us (4%)
    all_to_all x2, waiting for transfers between devices, swap_blocks(): return lax.all_to_all(blocks, axis, 0, 0, tiled=True)  75.2 us
    all_to_all x2, blocking collectives, swap_blocks(): return lax.all_to_all(blocks, axis, 0, 0, tiled=True)  69.2 us
    all_gather x1, blocking collectives, shards(): q_whole = lax.all_gather(q_init, 'tensor', axis=0, tiled=True)  23.1 us
    all_to_all x2, starting transfers between devices, swap_blocks(): return lax.all_to_all(blocks, axis, 0, 0, tiled=True)  13.2 us
    another operation x3, other arithmetic, shards(): low = jnp.linalg.cholesky(gram)  12.4 us
    another operation x2, other arithmetic, shards(): lax.linalg.triangular_solve(low, jnp.concatenate([p_sum, s_sum], axis=0),...  10.5 us
    dot_general x3, matrix products, dot_rows(): lax.dot_general(a, b, (((0,), (0,)), ((), ())), preferred_element_type=F32)  8.09 us
  transfers between devices with their start and end apart: 2, of which 2 were waited for; matrix products, arithmetic and copies ran while one was open for 0% of the time, Pallas kernels for 0%

profile of v1, /device:TPU:1, one launch (start us, length us, event | category | flops | bytes accessed | tf_op | source)
XLA Modules:
  0.0 232.3 jit_solution(4250787343292143624)
XLA Ops:
  0.7 23.1 %all_gather.3 = bf16[2304,128]{1,0:T(8,128)(2,1)S(1)} all-gather(bf16[144,128]{1,0:T(8,128)(2,1)} %param.6), channel_id=1, replica_groups=mesh['dp'=32,'tensor'=16] {'tensor'}, dimensions={0}, use_global_device_ids=true | all-gather | bytes 626688 | tf_op jit(solution)/shard_map/all_gather | solution.py:32
  23.8 3.0 %fusion.14 = f32[128,1152]{1,0:T(8,128)} fusion(bf16[256,1152]{1,0:T(8,128)(2,1)} %param.4, bf16[256,2304]{1,0:T(8,128)(2,1)} %param.5, bf16[2304,128]{1,0:T(8,128)(2,1)S(1)} %all_gather.3), kind=kOutput, calls=%fused_computation.14 | convolution fusion | flops 226525184 | bytes 2949120 | tf_op jit(solution)/shard_map/dot_general | solution.py:19
  26.8 2.8 %fusion.8 = f32[1152,128]{0,1:T(8,128)} fusion(f32[128,1152]{1,0:T(8,128)} %fusion.14, bf16[1,1152,1152]{2,1,0:T(8,128)(2,1)S(1)} %copy-done, bf16[2304,128]{1,0:T(8,128)(2,1)S(1)} %all_gather.3, s32[]{:T(128)S(6)} %select_n.30), kind=kOutput, calls=%fused_computation.7 | convolution fusion | flops 339886080 | bytes 4128772 | tf_op jit(solution)/shard_map/dot_general | solution.py:35
  29.6 1.3 copy.11
  30.9 27.2 %all_to_all.20 = f32[32,40,128]{2,1,0:T(8,128)S(1)} all-to-all(f32[32,40,128]{2,1,0:T(8,128)S(1)} %bitcast.45), channel_id=1, replica_groups=mesh['dp'=32,'tensor'=16] {'dp'}, dimensions={0} | all-to-all | bytes 1310720 | tf_op jit(solution)/shard_map/all_to_all | solution.py:11
  58.2 0.9 broadcast_in_dim.12
  59.1 8.2 %all-to-all-start.1 = ((f32[32,40,128]{2,1,0:T(8,128)}), f32[32,40,128]{2,1,0:T(8,128)S(1)}, u32[]{:S(2)}, u32[]{:S(2)}) async-start(f32[32,40,128]{2,1,0:T(8,128)} %broadcast_in_dim.12), calls=%async_computation.1 | async-start | bytes 1310720 | tf_op jit(solution)/shard_map/all_to_all | solution.py:11
  67.4 16.6 %all-to-all-done.1 = f32[32,40,128]{2,1,0:T(8,128)S(1)} async-done(((f32[32,40,128]{2,1,0:T(8,128)}), f32[32,40,128]{2,1,0:T(8,128)S(1)}, u32[]{:S(2)}, u32[]{:S(2)}) %all-to-all-start.1) | async-done | bytes 655392 | tf_op jit(solution)/shard_map/all_to_all | solution.py:11
  84.0 1.1 fusion.28
  85.1 1.5 fusion.11
  86.5 3.6 %fusion = f32[2304,128]{0,1:T(8,128)} fusion(bf16[256,2304]{1,0:T(8,128)(2,1)} %param.5, f32[1152,128]{0,1:T(8,128)} %fusion.11, bf16[256,1152]{1,0:T(8,128)(2,1)} %param.4, pred[]{:T(512)S(6)} %eq.5, f32[1280,128]{1,0:T(8,128)S(1)} %bitcast.42), kind=kOutput, calls=%fused_computation.1 | convolution fusion | flops 227115008 | bytes 3833857 | tf_op jit(solution)/shard_map/dot_general | solution.py:19
  90.2 2.7 %copy.9 = f32[2304,128]{1,0:T(8,128)} copy(f32[2304,128]{0,1:T(8,128)} %fusion) | data formatting | bytes 2359296 | tf_op jit(solution)/shard_map/add | solution.py:48
  92.9 1.4 pad_maximum_fusion
  94.2 41.9 %all_to_all.21 = f32[16,152,128]{2,1,0:T(8,128)} all-to-all(f32[16,152,128]{2,1,0:T(8,128)S(1)} %pad_maximum_fusion), channel_id=1, replica_groups=mesh['dp'=32,'tensor'=16] {'tensor'}, dimensions={0} | all-to-all | bytes 2490368 | tf_op jit(solution)/shard_map/all_to_all | solution.py:11
  136.2 1.4 reduce_sum.28
  137.5 1.6 broadcast_in_dim.14
  139.2 5.0 %all-to-all-start.3 = ((f32[32,152,128]{2,1,0:T(8,128)}), f32[32,152,128]{2,1,0:T(8,128)}, u32[]{:S(2)}, u32[]{:S(2)}) async-start(f32[32,152,128]{2,1,0:T(8,128)} %broadcast_in_dim.14), calls=%async_computation.3 | async-start | bytes 4980736 | tf_op jit(solution)/shard_map/all_to_all | solution.py:11
  144.2 0.9 slice.30
  145.0 58.7 %all-to-all-done.3 = f32[32,152,128]{2,1,0:T(8,128)} async-done(((f32[32,152,128]{2,1,0:T(8,128)}), f32[32,152,128]{2,1,0:T(8,128)}, u32[]{:S(2)}, u32[]{:S(2)}) %all-to-all-start.3) | async-done | bytes 2490400 | tf_op jit(solution)/shard_map/all_to_all | solution.py:11
  203.7 0.8 slice_bitcast_fusion
  204.6 0.9 fusion.24
  205.5 11.7 %cholesky.16 = f32[128,128]{1,0:T(8,128)S(1)} custom-call(f32[128,128]{1,0:T(8,128)S(1)} %fusion.24), custom_call_target="Cholesky" | custom-call | tf_op jit(solution)/shard_map/jit(cholesky)/cholesky | solution.py:69
  217.2 1.9 slice_reduce_fusion
  220.4 9.8 %custom-call.6 = f32[1,128,128]{1,2,0:T(8,128)S(1)} custom-call(f32[1,128,128]{2,1,0:T(8,128)S(1)} %fusion.22), custom_call_target="InvertDiagBlocksLowerTriangular" | custom-call | tf_op jit(solution)/shard_map/triangular_solve | solution.py:70
  (17 shorter events, 3.6 us)
Async XLA Ops:
  0.6 26.2 %copy-start = (bf16[1,1152,1152]{2,1,0:T(8,128)(2,1)S(1)}, bf16[1,1152,1152]{2,1,0:T(8,128)(2,1)}, u32[]{:S(2)}) copy-start(bf16[1,1152,1152]{2,1,0:T(8,128)(2,1)} %param.7) | copy-start | bytes 7962628
  59.1 24.9 %all-to-all-start.1 = ((f32[32,40,128]{2,1,0:T(8,128)}), f32[32,40,128]{2,1,0:T(8,128)S(1)}, u32[]{:S(2)}, u32[]{:S(2)}) async-start(f32[32,40,128]{2,1,0:T(8,128)} %broadcast_in_dim.12), calls=%async_computation.1 | async-start | bytes 1310720 | tf_op jit(solution)/shard_map/all_to_all | solution.py:11
  139.2 64.5 %all-to-all-start.3 = ((f32[32,152,128]{2,1,0:T(8,128)}), f32[32,152,128]{2,1,0:T(8,128)}, u32[]{:S(2)}, u32[]{:S(2)}) async-start(f32[32,152,128]{2,1,0:T(8,128)} %broadcast_in_dim.14), calls=%async_computation.3 | async-start | bytes 4980736 | tf_op jit(solution)/shard_map/all_to_all | solution.py:11
  217.2 13.0 %copy-start.1 = (f32[1152,128]{1,0:T(8,128)S(1)}, f32[1152,128]{1,0:T(8,128)}, u32[]{:S(2)}) copy-start(f32[1152,128]{1,0:T(8,128)} %slice.30) | copy-start | bytes 1769476

commit v2 on v1

v2 whole, which is shorter than its diff:
```python
import functools

import jax
import jax.numpy as jnp
from jax import lax
from jax.experimental import pallas as pl
from jax.experimental.pallas import tpu as pltpu
from jax.sharding import Mesh
from jax.sharding import PartitionSpec as P

F32 = jnp.float32
BF16 = jnp.bfloat16
DP = ("x", "z")
TENSOR = ("y", "core")
VMEM_BYTES = 32 * 2**20
STEP = 8


def swap_blocks(blocks, axis):
    return lax.all_to_all(blocks, axis, 0, 0, tiled=True)


def dot(a, b):
    return jnp.dot(a, b, preferred_element_type=F32)


def dot_rows(a, b):
    return lax.dot_general(a, b, (((0,), (0,)), ((), ())), preferred_element_type=F32)


def dot_cols(a, b):
    return lax.dot_general(a, b, (((1,), (1,)), ((), ())), preferred_element_type=F32)


def round_up(count, multiple):
    return -(-count // multiple) * multiple


def two_terms(value):
    high = value.astype(BF16)
    rest = (value - high.astype(F32)).astype(BF16)
    return high, rest


def three_terms(value):
    high = value.astype(BF16)
    rest = value - high.astype(F32)
    middle = rest.astype(BF16)
    low = (rest - middle.astype(F32)).astype(BF16)
    return high.astype(F32), middle.astype(F32), low.astype(F32)


def call(kernel, out_shapes, scratch, flops, bytes_accessed, in_specs):
    return pl.pallas_call(
        kernel,
        out_shape=out_shapes,
        in_specs=in_specs,
        scratch_shapes=scratch,
        compiler_params=pltpu.CompilerParams(vmem_limit_bytes=VMEM_BYTES),
        cost_estimate=pl.CostEstimate(flops=flops, bytes_accessed=bytes_accessed, transcendentals=0),
    )


IN_VMEM = pl.BlockSpec(memory_space=pltpu.VMEM)
IN_SMEM = pl.BlockSpec(memory_space=pltpu.SMEM)
ANYWHERE = pl.BlockSpec(memory_space=pl.ANY)


def fetch(sources, targets, sems):
    copies = []
    for index, (source, target) in enumerate(zip(sources, targets)):
        copies.append(pltpu.make_async_copy(source, target, sems.at[index]))
        copies[-1].start()
    return copies


def left_term_kernel(cuts, place_ref, hid_hbm, out_hbm, err_hbm, q_ref, o_ref, hid, out, err, sems):
    rows = hid.shape[1]
    half = err.shape[1]
    slab = rows // cuts
    sources = [out_hbm, hid_hbm] + [err_hbm.at[0, pl.ds(i * slab, slab)] for i in range(cuts)]
    targets = [out, hid] + [err.at[pl.ds(i * slab, slab)] for i in range(cuts)]
    copies = fetch(sources, targets, sems)
    copies[0].wait()
    high, rest = two_terms(dot(out[...], q_ref[...]))
    both = jnp.concatenate([high, rest], axis=1)
    copies[1].wait()
    turned = dot_rows(both, hid[...])
    rank = high.shape[1]
    turned = jnp.transpose(turned[:rank] + turned[rank:])
    side = place_ref[1] % 2
    q_mine = q_ref[pl.ds(pl.multiple_of(side * half, 128), half), :]
    terms = []
    for i in range(cuts):
        copies[2 + i].wait()
        part = dot(err[pl.ds(i * slab, slab), :], q_mine)
        terms.append(part + turned[i * slab : (i + 1) * slab])
    term = jnp.concatenate(terms, axis=0)
    blocks, chunk, _ = o_ref.shape
    for i in range(blocks):
        piece = term[min(i * chunk, rows) : min((i + 1) * chunk, rows)]
        missing = chunk - piece.shape[0]
        if missing == chunk:
            piece = jnp.zeros((chunk, rank), F32)
        elif missing:
            piece = jnp.concatenate([piece, jnp.zeros((missing, rank), F32)], axis=0)
        o_ref[i] = piece.astype(BF16)


def left_term(place, hidden, grad_out, error, q_whole, blocks, chunk):
    tokens, rows = hidden.shape
    width, rank = q_whole.shape
    half = error.shape[2]
    cuts = 4
    return call(
        functools.partial(left_term_kernel, cuts),
        jax.ShapeDtypeStruct((blocks, chunk, rank), BF16),
        [
            pltpu.VMEM((tokens, rows), BF16),
            pltpu.VMEM((tokens, width), BF16),
            pltpu.VMEM((rows, half), BF16),
            pltpu.SemaphoreType.DMA((2 + cuts,)),
        ],
        2 * rank * (tokens * (width + rows) + rows * half),
        2 * (tokens * (width + rows) + rows * half + width * rank),
        [IN_SMEM, ANYWHERE, ANYWHERE, ANYWHERE, IN_VMEM],
    )(place, hidden, grad_out, error, q_whole)


def mean_kernel(scale, in_ref, o_ref):
    blocks = in_ref.shape[0]
    total = in_ref[0].astype(F32)
    for i in range(1, blocks):
        total += in_ref[i].astype(F32)
    total = (total * scale).astype(BF16)
    for i in range(blocks):
        o_ref[i] = total


def mean_of_blocks(blocks, scale):
    return call(
        functools.partial(mean_kernel, scale),
        jax.ShapeDtypeStruct(blocks.shape, BF16),
        [],
        blocks.size,
        4 * blocks.size,
        [IN_VMEM],
    )(blocks)


def packet_kernel(n_x, n_z, cuts, place_ref, hid_hbm, out_hbm, err_hbm, p_ref, o_ref, hid, out, err, turned, flat, pack, gram, sems):
    tokens, rows = hid.shape
    width = out.shape[1]
    half = err.shape[1]
    rank = p_ref.shape[1]
    slab = rows // cuts
    sources = [hid_hbm] + [err_hbm.at[0, pl.ds(i * slab, slab)] for i in range(cuts)] + [out_hbm]
    targets = [hid] + [err.at[pl.ds(i * slab, slab)] for i in range(cuts)] + [out]
    copies = fetch(sources, targets, sems)
    x, z = place_ref[0], place_ref[1]
    quarter = rows // n_x
    p_quarter = p_ref[pl.ds(pl.multiple_of(x * quarter, 16), quarter), :]
    gram[...] = dot_rows(p_quarter, p_quarter)
    copies[0].wait()
    high, rest = two_terms(dot(hid[...], p_ref[:rows, :]))
    both = jnp.concatenate([high, rest], axis=1)
    from_err = jnp.zeros((rank, half), F32)
    for i in range(cuts):
        copies[1 + i].wait()
        from_err += dot_rows(p_ref[i * slab : (i + 1) * slab, :], err[pl.ds(i * slab, slab), :])
    copies[1 + cuts].wait()
    from_out = dot_rows(both, out[...])
    turned[...] = from_out[:rank] + from_out[rank:]
    side = z % 2
    mine = pl.ds(pl.multiple_of(side * half, 128), half)
    turned[:, mine] += from_err
    for i in range(width // rank):
        flat[i * rank : (i + 1) * rank, :] = jnp.transpose(turned[:, i * rank : (i + 1) * rank])
    count = o_ref.shape[0]
    piece = width // count
    few = rank // (n_x * n_z)
    own = gram[pl.ds(pl.multiple_of(z * (few * n_x), 8), few * n_x), :]
    terms = three_terms(own)
    for i in range(count):
        at = i % n_x
        pack[i, 0:piece, :] = flat[i * piece : (i + 1) * piece, :]
        for j, term in enumerate(terms):
            pack[i, piece + j * few : piece + (j + 1) * few, :] = term[at * few : (at + 1) * few]
    o_ref[...] = pack[...].astype(BF16)


def packets_of(place, hidden, grad_out, error, p_sum, n_x, n_z, n_tensor):
    tokens, rows = hidden.shape
    width = grad_out.shape[1]
    half = error.shape[2]
    rank = p_sum.shape[1]
    cuts = 4
    count = n_tensor * n_x
    deep = width // count + 3 * (rank // (n_x * n_z))
    return call(
        functools.partial(packet_kernel, n_x, n_z, cuts),
        jax.ShapeDtypeStruct((count, deep, rank), BF16),
        [
            pltpu.VMEM((tokens, rows), BF16),
            pltpu.VMEM((tokens, width), BF16),
            pltpu.VMEM((rows, half), BF16),
            pltpu.VMEM((rank, width), F32),
            pltpu.VMEM((width, rank), F32),
            pltpu.VMEM((count, deep, rank), F32),
            pltpu.VMEM((rank, rank), F32),
            pltpu.SemaphoreType.DMA((2 + cuts,)),
        ],
        2 * rank * (tokens * (width + rows) + rows * half),
        2 * (tokens * (width + rows) + rows * half + rows * rank),
        [IN_SMEM, ANYWHERE, ANYWHERE, ANYWHERE, IN_VMEM],
    )(place, hidden, grad_out, error, p_sum)


def repack_kernel(few, in_ref, o_ref, pack):
    count, deep, rank = in_ref.shape
    piece = deep - 3 * few
    total = in_ref[0].astype(F32)
    for i in range(1, count):
        total += in_ref[i].astype(F32)
    pack[...] = total
    rows = [pack[piece + j * few : piece + (j + 1) * few, :] for j in range(3)]
    for j, term in enumerate(three_terms((rows[2] + rows[1]) + rows[0])):
        pack[piece + j * few : piece + (j + 1) * few, :] = term
    packet = pack[...].astype(BF16)
    for i in range(o_ref.shape[0]):
        o_ref[i] = packet


def repacked(packets, few, n_dp):
    count, deep, rank = packets.shape
    return call(
        functools.partial(repack_kernel, few),
        jax.ShapeDtypeStruct((n_dp, deep, rank), BF16),
        [pltpu.VMEM((deep, rank), F32)],
        packets.size,
        4 * packets.size,
        [IN_VMEM],
    )(packets)


def small_factor(block, like):
    size = block.shape[0]
    a = {}
    for i in range(size):
        for j in range(i + 1):
            a[i, j] = jnp.broadcast_to(block[i : i + 1, j : j + 1], like)
    inverse = {}
    for j in range(size):
        pivot = a[j, j]
        scale = lax.rsqrt(pivot)
        scale = scale * (1.5 - (0.5 * pivot) * (scale * scale))
        for m in range(j):
            inverse[j, m] = inverse[j, m] * scale
        inverse[j, j] = scale
        column = {i: a[i, j] * scale for i in range(j + 1, size)}
        for i in range(j + 1, size):
            for m in range(j + 1, i + 1):
                a[i, m] = a[i, m] - column[i] * column[m]
            for m in range(j + 1):
                step = column[i] * inverse[j, m]
                inverse[i, m] = inverse[i, m] - step if (i, m) in inverse else -step
    return inverse


def inverse_factor(gram):
    rank = gram.shape[0]
    like = (STEP, rank)
    lane = lax.broadcasted_iota(jnp.int32, like, 1)
    tiles = [gram[b * STEP : (b + 1) * STEP, :] for b in range(rank // STEP)]
    done = []
    for k in range(rank // STEP):
        first = k * STEP
        inverse = small_factor(tiles[k][:, first : first + STEP], like)
        inside = (lane >= first) & (lane < first + STEP)
        pivots = []
        for m in range(STEP):
            row = jnp.broadcast_to(tiles[k][m : m + 1, :], like)
            pivots.append(jnp.where(inside, jnp.where(lane == first + m, 1.0, 0.0), row))
        scaled = []
        for i in range(STEP):
            row = inverse[i, 0] * pivots[0]
            for m in range(1, i + 1):
                row = row + inverse[i, m] * pivots[m]
            scaled.append(row)
        sublane = lax.broadcasted_iota(jnp.int32, like, 0)
        rows = scaled[0]
        for i in range(1, STEP):
            rows = jnp.where(sublane == i, scaled[i], rows)
        done.append(jnp.where(lane <= first + sublane, rows, 0.0))
        for b in range(k + 1, rank // STEP):
            columns = [
                jnp.broadcast_to(tiles[b][:, first + m : first + m + 1], like) for m in range(STEP)
            ]
            tile = jnp.where(inside, 0.0, tiles[b])
            for i in range(STEP):
                factor = inverse[i, 0] * columns[0]
                for m in range(1, i + 1):
                    factor = factor + inverse[i, m] * columns[m]
                tile = tile - factor * scaled[i]
            tiles[b] = tile
    return jnp.concatenate(done, axis=0)


def finish_kernel(scale, pick_ref, in_ref, p_ref, p_out, q_out):
    rank = p_ref.shape[1]
    summed = dot(pick_ref[...], in_ref[...])
    inverse = inverse_factor(summed[:rank])
    s_sum = summed[rank:] * scale
    terms = [term.astype(BF16) for term in three_terms(inverse)]
    p_low = p_ref[: p_out.shape[0], :]
    p_new = dot_cols(p_low, terms[2]) + dot_cols(p_low, terms[1])
    p_out[...] = (p_new + dot_cols(p_low, terms[0])).astype(BF16)
    q_new = lax.dot_general(
        s_sum,
        inverse,
        (((1,), (1,)), ((), ())),
        precision=lax.Precision.HIGHEST,
        preferred_element_type=F32,
    )
    q_out[...] = q_new.astype(BF16)


def pick_rows(n_x, n_z, piece, few, rank):
    deep = piece + 3 * few
    count = n_x * n_z
    source = lax.broadcasted_iota(jnp.int32, (1, count * deep), 1)
    device, row = source // deep, source % deep
    x, z = device // n_z, device % n_z
    gram_row = z * (few * n_x) + x * few + (row - piece) % few
    factor_row = rank + x * piece + row
    target = jnp.where(row < piece, factor_row, gram_row)
    rows = lax.broadcasted_iota(jnp.int32, (rank + n_x * piece, 1), 0)
    return (rows == target).astype(BF16)


def finished(packets, p_sum, rows, n_x, n_z, few):
    count, deep, rank = packets.shape
    piece = deep - 3 * few
    pick = pick_rows(n_x, n_z, piece, few, rank)
    return call(
        functools.partial(finish_kernel, 2.0 / count),
        (
            jax.ShapeDtypeStruct((rows, rank), BF16),
            jax.ShapeDtypeStruct((n_x * piece, rank), BF16),
        ),
        [],
        2 * rank * (pick.size + 3 * rows * rank),
        2 * (pick.size + 2 * rows * rank),
        [IN_VMEM, IN_VMEM, IN_VMEM],
    )(pick, packets.reshape(count * deep, rank), p_sum)


def shards(hidden, grad_out, q_init, error):
    n_x, n_z = lax.axis_size("x"), lax.axis_size("z")
    n_dp, n_tensor = lax.axis_size(DP), lax.axis_size(TENSOR)
    replicas = n_dp // 2
    place = jnp.stack([lax.axis_index("x"), lax.axis_index("z")]).astype(jnp.int32)
    rows, rank = hidden.shape[1], q_init.shape[1]
    few = rank // n_dp
    chunk = round_up(-(-rows // n_dp), 8)

    q_whole = lax.all_gather(q_init, TENSOR, axis=0, tiled=True)
    pieces = left_term(place, hidden, grad_out, error, q_whole, n_dp, chunk)
    pieces = mean_of_blocks(swap_blocks(pieces, DP), 1.0 / replicas)
    p_sum = swap_blocks(pieces, DP).reshape(n_dp * chunk, rank)
    packets = packets_of(place, hidden, grad_out, error, p_sum, n_x, n_z, n_tensor)
    packets = repacked(swap_blocks(packets, TENSOR + ("x",)), few, n_dp)
    return finished(swap_blocks(packets, DP), p_sum, rows, n_x, n_z, few)


def solution(mesh):
    fine = Mesh(mesh.devices.reshape(4, 8, 8, 2), DP + TENSOR)
    in_specs = (P(DP, TENSOR), P(DP, None), P(TENSOR, None), P(DP, TENSOR, None))
    out_specs = (P(TENSOR, None), P(TENSOR, None))
    return jax.shard_map(shards, mesh=fine, in_specs=in_specs, out_specs=out_specs, check_vma=False)
```

time: 233 us -> 137 us (0.59)
  the two profiles are of different devices: /device:TPU:1 before, /device:TPU:64 now
where the time goes in v2:
time: 137 us; the launch traced here: 136 us
  blocking collectives  93.1 us (68%)
  Pallas kernels  17.8 us (13%)
  waiting for transfers between devices  14.2 us (10%)
  starting transfers between devices  6.23 us (5%)
  local copies, waits for them, and re-layouts  4.1 us (3%)
    all_to_all x3, blocking collectives, swap_blocks(): return lax.all_to_all(blocks, axis, 0, 0, tiled=True)  73.7 us
    all_gather x1, blocking collectives, shards(): q_whole = lax.all_gather(q_init, TENSOR, axis=0, tiled=True)  19.4 us
    all_to_all x1, waiting for transfers between devices, swap_blocks(): return lax.all_to_all(blocks, axis, 0, 0, tiled=True)  14.2 us
    pallas_call x1, Pallas kernels, finished(): call(functools.partial(finish_kernel, 2.0 / count), (jax.ShapeDtypeStruct...  7.55 us
    all_to_all x1, starting transfers between devices, swap_blocks(): return lax.all_to_all(blocks, axis, 0, 0, tiled=True)  6.23 us
    pallas_call x1, Pallas kernels, packets_of(): call(functools.partial(packet_kernel, n_x, n_z, cuts), jax.ShapeDtypeStru...  4.69 us
    pallas_call x1, Pallas kernels, left_term(): call(functools.partial(left_term_kernel, cuts), jax.ShapeDtypeStruct((blo...  4.62 us
    unnamed x10, local copies, waits for them, and re-layouts  4.1 us
  transfers between devices with their start and end apart: 1, of which 1 were waited for; matrix products, arithmetic and copies ran while one was open for 0% of the time, Pallas kernels for 0%

profile of v2, /device:TPU:64, one launch (start us, length us, event | category | flops | bytes accessed | tf_op | source)
XLA Modules:
  0.0 136.5 jit_solution(11578080869204836732)
XLA Ops:
  0.6 19.4 %all_gather.3.q_ref = bf16[2304,128]{1,0:T(8,128)(2,1)S(1)} all-gather(bf16[144,128]{1,0:T(8,128)(2,1)} %param.6), channel_id=1, replica_groups=mesh['x'=4,'z'=8,'y'=8,'core'=2] {'y','core'}, dimensions={0}, use_global_device_ids=true | all-gather | bytes 626688 | tf_op jit(solution)/shard_map/all_gather | solution.py:367
  20.1 0.1 pad_add_fusion.place_ref
  20.2 0.0 copy-start
  20.2 1.7 %copy-done = bf16[1,1152,1152]{2,1,0:T(8,128)(2,1)S(1)} copy-done((bf16[1,1152,1152]{2,1,0:T(8,128)(2,1)S(1)}, bf16[1,1152,1152]{2,1,0:T(8,128)(2,1)}, u32[]{:S(2)}) %copy-start) | copy-done | bytes 2654232
  21.9 0.0 copy-start.1
  21.9 1.3 copy-done.1
  23.2 0.0 copy-start.3
  23.2 1.1 copy-done.3
  24.2 4.6 %shard_map.59 = bf16[32,40,128]{2,1,0:T(8,128)(2,1)S(1)} custom-call(s32[2]{0:T(128)S(1)} %pad_add_fusion.place_ref, bf16[256,1152]{1,0:T(8,128)(2,1)S(1)} %copy-done.3, bf16[256,2304]{1,0:T(8,128)(2,1)S(1)} %copy-done.1, bf16[1,1152,1152]{2,1,0:T(8,128)(2,1)S(1)} %copy-done, bf16[2304,128]{1,0:T(8,128)(2,1)S(1)} %all_gather.3.q_ref), custom_call_target="tpu_custom_call" | custom-call | flops 566231040 | bytes 5013504 | tf_op jit(solution)/shard_map/pallas_call | solution.py:115
  28.9 0.0 copy-start.2
  28.9 0.0 copy-start.4
  28.9 26.6 %all_to_all.20.in_ref = bf16[32,40,128]{2,1,0:T(8,128)(2,1)S(1)} all-to-all(bf16[32,40,128]{2,1,0:T(8,128)(2,1)S(1)} %shard_map.59), channel_id=1, replica_groups=mesh['x'=4,'z'=8,'y'=8,'core'=2] {'x','z'}, dimensions={0} | all-to-all | bytes 655360 | tf_op jit(solution)/shard_map/all_to_all | solution.py:20
  55.5 0.1 shard_map.60
  55.6 17.8 %all_to_all.21 = bf16[32,40,128]{2,1,0:T(8,128)(2,1)S(1)} all-to-all(bf16[32,40,128]{2,1,0:T(8,128)(2,1)S(1)} %shard_map.60), channel_id=1, replica_groups=mesh['x'=4,'z'=8,'y'=8,'core'=2] {'x','z'}, dimensions={0} | all-to-all | bytes 655360 | tf_op jit(solution)/shard_map/all_to_all | solution.py:20
  73.4 0.0 copy-done.2
  73.4 0.0 copy-done.4
  73.4 4.7 %shard_map.61 = bf16[64,48,128]{2,1,0:T(8,128)(2,1)S(1)} custom-call(s32[2]{0:T(128)S(1)} %pad_add_fusion.place_ref, bf16[256,1152]{1,0:T(8,128)(2,1)S(1)} %copy-done.4, bf16[256,2304]{1,0:T(8,128)(2,1)S(1)} %copy-done.2, bf16[1,1152,1152]{2,1,0:T(8,128)(2,1)S(1)} %copy-done, bf16[1280,128]{1,0:T(8,128)(2,1)S(1)} %bitcast.4), custom_call_target="tpu_custom_call" | custom-call | flops 566231040 | bytes 4718592 | tf_op jit(solution)/shard_map/pallas_call | solution.py:200
  78.1 29.2 %all_to_all.22.in_ref = bf16[64,48,128]{2,1,0:T(8,128)(2,1)S(1)} all-to-all(bf16[64,48,128]{2,1,0:T(8,128)(2,1)S(1)} %shard_map.61), channel_id=1, replica_groups=mesh['x'=4,'z'=8,'y'=8,'core'=2] {'y','core','x'}, dimensions={0} | all-to-all | bytes 1572864 | tf_op jit(solution)/shard_map/all_to_all | solution.py:20
  107.4 0.9 shard_map.62
  108.3 6.2 %all-to-all-start.3 = ((bf16[32,48,128]{2,1,0:T(8,128)(2,1)}), bf16[32,48,128]{2,1,0:T(8,128)(2,1)S(1)}, u32[]{:S(2)}, u32[]{:S(2)}) async-start(bf16[32,48,128]{2,1,0:T(8,128)(2,1)} %shard_map.62), calls=%async_computation.3 | async-start | bytes 786432 | tf_op jit(solution)/shard_map/all_to_all | solution.py:20
  114.5 0.2 fusion.pick_ref
  114.7 14.2 %all-to-all-done.3 = bf16[32,48,128]{2,1,0:T(8,128)(2,1)S(1)} async-done(((bf16[32,48,128]{2,1,0:T(8,128)(2,1)}), bf16[32,48,128]{2,1,0:T(8,128)(2,1)S(1)}, u32[]{:S(2)}, u32[]{:S(2)}) %all-to-all-start.3) | async-done | bytes 393248 | tf_op jit(solution)/shard_map/all_to_all | solution.py:20
  128.9 7.6 %shard_map.63 = (bf16[1152,128]{1,0:T(8,128)(2,1)}, bf16[144,128]{1,0:T(8,128)(2,1)}) custom-call(bf16[272,1536]{1,0:T(8,128)(2,1)S(1)} %fusion.pick_ref, bf16[1536,128]{1,0:T(8,128)(2,1)S(1)} %bitcast.6, bf16[1280,128]{1,0:T(8,128)(2,1)S(1)} %bitcast.5), custom_call_target="tpu_custom_call" | custom-call | flops 220200960 | bytes 1425408 | tf_op jit(solution)/shard_map/pallas_call | solution.py:345
  (1 shorter events, 0.0 us)
Async XLA Ops:
  20.2 1.8 %copy-start = (bf16[1,1152,1152]{2,1,0:T(8,128)(2,1)S(1)}, bf16[1,1152,1152]{2,1,0:T(8,128)(2,1)}, u32[]{:S(2)}) copy-start(bf16[1,1152,1152]{2,1,0:T(8,128)(2,1)} %err_hbm.3) | copy-start | bytes 7962628
  21.9 1.3 copy-start.1
  23.2 1.1 copy-start.3
  28.9 44.5 %copy-start.2 = (bf16[256,2304]{1,0:T(8,128)(2,1)S(1)}, bf16[256,2304]{1,0:T(8,128)(2,1)}, u32[]{:S(2)}) copy-start(bf16[256,2304]{1,0:T(8,128)(2,1)} %out_hbm.3) | copy-start | bytes 3538948
  28.9 44.5 %copy-start.4 = (bf16[256,1152]{1,0:T(8,128)(2,1)S(1)}, bf16[256,1152]{1,0:T(8,128)(2,1)}, u32[]{:S(2)}) copy-start(bf16[256,1152]{1,0:T(8,128)(2,1)} %hid_hbm.3) | copy-start | bytes 1769476
  108.3 20.6 %all-to-all-start.3 = ((bf16[32,48,128]{2,1,0:T(8,128)(2,1)}), bf16[32,48,128]{2,1,0:T(8,128)(2,1)S(1)}, u32[]{:S(2)}, u32[]{:S(2)}) async-start(bf16[32,48,128]{2,1,0:T(8,128)(2,1)} %shard_map.62), calls=%async_computation.3 | async-start | bytes 786432 | tf_op jit(solution)/shard_map/all_to_all | solution.py:20

commit v3 on v2

--- a/solution.py
+++ b/solution.py
@@ -13,6 +13,7 @@
 DP = ("x", "z")
 TENSOR = ("y", "core")
 VMEM_BYTES = 32 * 2**20
+VMEM_MOST = 53 * 2**20
 STEP = 8
 
 
@@ -50,19 +51,18 @@
     return high.astype(F32), middle.astype(F32), low.astype(F32)
 
 
-def call(kernel, out_shapes, scratch, flops, bytes_accessed, in_specs):
+def call(kernel, out_shapes, scratch, flops, bytes_accessed, in_specs, vmem=VMEM_BYTES):
     return pl.pallas_call(
         kernel,
         out_shape=out_shapes,
         in_specs=in_specs,
         scratch_shapes=scratch,
-        compiler_params=pltpu.CompilerParams(vmem_limit_bytes=VMEM_BYTES),
+        compiler_params=pltpu.CompilerParams(vmem_limit_bytes=vmem),
         cost_estimate=pl.CostEstimate(flops=flops, bytes_accessed=bytes_accessed, transcendentals=0),
     )
 
 
 IN_VMEM = pl.BlockSpec(memory_space=pltpu.VMEM)
-IN_SMEM = pl.BlockSpec(memory_space=pltpu.SMEM)
 ANYWHERE = pl.BlockSpec(memory_space=pl.ANY)
 
 
@@ -74,28 +74,46 @@
     return copies
 
 
-def left_term_kernel(cuts, place_ref, hid_hbm, out_hbm, err_hbm, q_ref, o_ref, hid, out, err, sems):
-    rows = hid.shape[1]
-    half = err.shape[1]
-    slab = rows // cuts
-    sources = [out_hbm, hid_hbm] + [err_hbm.at[0, pl.ds(i * slab, slab)] for i in range(cuts)]
-    targets = [out, hid] + [err.at[pl.ds(i * slab, slab)] for i in range(cuts)]
-    copies = fetch(sources, targets, sems)
+def token_term_kernel(hid_hbm, out_hbm, q_hbm, o_ref, own_ref, hid, out, q, sems):
+    rank = q.shape[1]
+    half = own_ref.shape[0]
+    copies = fetch([q_hbm, out_hbm, hid_hbm], [q, out, hid], sems)
+    side = lax.axis_index("z") % 2
     copies[0].wait()
-    high, rest = two_terms(dot(out[...], q_ref[...]))
+    own_ref[...] = q[pl.ds(pl.multiple_of(side * half, 128), half), :]
+    copies[1].wait()
+    high, rest = two_terms(dot(out[...], q[...]))
     both = jnp.concatenate([high, rest], axis=1)
-    copies[1].wait()
-    turned = dot_rows(both, hid[...])
-    rank = high.shape[1]
-    turned = jnp.transpose(turned[:rank] + turned[rank:])
-    side = place_ref[1] % 2
-    q_mine = q_ref[pl.ds(pl.multiple_of(side * half, 128), half), :]
-    terms = []
-    for i in range(cuts):
-        copies[2 + i].wait()
-        part = dot(err[pl.ds(i * slab, slab), :], q_mine)
-        terms.append(part + turned[i * slab : (i + 1) * slab])
-    term = jnp.concatenate(terms, axis=0)
+    copies[2].wait()
+    turned = dot_rows(hid[...], both)
+    o_ref[...] = turned[:, :rank] + turned[:, rank:]
+
+
+def token_term(hidden, grad_out, q_whole, half):
+    tokens, rows = hidden.shape
+    width, rank = q_whole.shape
+    return call(
+        token_term_kernel,
+        (
+            jax.ShapeDtypeStruct((rows, rank), F32),
+            jax.ShapeDtypeStruct((half, rank), BF16),
+        ),
+        [
+            pltpu.VMEM((tokens, rows), BF16),
+            pltpu.VMEM((tokens, width), BF16),
+            pltpu.VMEM((width, rank), BF16),
+            pltpu.SemaphoreType.DMA((3,)),
+        ],
+        2 * rank * tokens * (width + 2 * rows),
+        2 * (tokens * (width + rows) + width * rank),
+        [ANYWHERE] * 3,
+        VMEM_MOST,
+    )(hidden, grad_out, q_whole)
+
+
+def left_term_kernel(err_ref, own_ref, token_ref, o_ref):
+    rows, rank = token_ref.shape
+    term = dot(err_ref[0], own_ref[...]) + token_ref[...]
     blocks, chunk, _ = o_ref.shape
     for i in range(blocks):
         piece = term[min(i * chunk, rows) : min((i + 1) * chunk, rows)]
@@ -107,24 +125,17 @@
         o_ref[i] = piece.astype(BF16)
 
 
-def left_term(place, hidden, grad_out, error, q_whole, blocks, chunk):
-    tokens, rows = hidden.shape
-    width, rank = q_whole.shape
+def left_term(error, q_own, tokens, blocks, chunk):
+    rows, rank = tokens.shape
     half = error.shape[2]
-    cuts = 4
-    return call(
-        functools.partial(left_term_kernel, cuts),
+    return call(
+        left_term_kernel,
         jax.ShapeDtypeStruct((blocks, chunk, rank), BF16),
-        [
-            pltpu.VMEM((tokens, rows), BF16),
-            pltpu.VMEM((tokens, width), BF16),
-            pltpu.VMEM((rows, half), BF16),
-            pltpu.SemaphoreType.DMA((2 + cuts,)),
-        ],
-        2 * rank * (tokens * (width + rows) + rows * half),
-        2 * (tokens * (width + rows) + rows * half + width * rank),
-        [IN_SMEM, ANYWHERE, ANYWHERE, ANYWHERE, IN_VMEM],
-    )(place, hidden, grad_out, error, q_whole)
+        [],
+        2 * rank * rows * half,
+        2 * (rows * half + half * rank),
+        [IN_VMEM] * 3,
+    )(error, q_own, tokens)
 
 
 def mean_kernel(scale, in_ref, o_ref):
@@ -148,72 +159,80 @@
     )(blocks)
 
 
-def packet_kernel(n_x, n_z, cuts, place_ref, hid_hbm, out_hbm, err_hbm, p_ref, o_ref, hid, out, err, turned, flat, pack, gram, sems):
-    tokens, rows = hid.shape
-    width = out.shape[1]
-    half = err.shape[1]
+def right_term_kernel(n_x, n_tensor, hid_ref, out_ref, err_ref, p_ref, send_ref, keep_ref, turned, flat, gram):
+    rows = hid_ref.shape[1]
+    width = out_ref.shape[1]
+    half = err_ref.shape[2]
     rank = p_ref.shape[1]
-    slab = rows // cuts
-    sources = [hid_hbm] + [err_hbm.at[0, pl.ds(i * slab, slab)] for i in range(cuts)] + [out_hbm]
-    targets = [hid] + [err.at[pl.ds(i * slab, slab)] for i in range(cuts)] + [out]
-    copies = fetch(sources, targets, sems)
-    x, z = place_ref[0], place_ref[1]
+    x, z, core = (lax.axis_index(axis) for axis in ("x", "z", "core"))
     quarter = rows // n_x
     p_quarter = p_ref[pl.ds(pl.multiple_of(x * quarter, 16), quarter), :]
     gram[...] = dot_rows(p_quarter, p_quarter)
-    copies[0].wait()
-    high, rest = two_terms(dot(hid[...], p_ref[:rows, :]))
+    p_own = p_ref[:rows, :]
+    high, rest = two_terms(dot(hid_ref[...], p_own))
     both = jnp.concatenate([high, rest], axis=1)
-    from_err = jnp.zeros((rank, half), F32)
-    for i in range(cuts):
-        copies[1 + i].wait()
-        from_err += dot_rows(p_ref[i * slab : (i + 1) * slab, :], err[pl.ds(i * slab, slab), :])
-    copies[1 + cuts].wait()
-    from_out = dot_rows(both, out[...])
+    from_err = dot_rows(p_own, err_ref[0])
+    from_out = dot_rows(both, out_ref[...])
     turned[...] = from_out[:rank] + from_out[rank:]
     side = z % 2
     mine = pl.ds(pl.multiple_of(side * half, 128), half)
     turned[:, mine] += from_err
     for i in range(width // rank):
         flat[i * rank : (i + 1) * rank, :] = jnp.transpose(turned[:, i * rank : (i + 1) * rank])
-    count = o_ref.shape[0]
-    piece = width // count
-    few = rank // (n_x * n_z)
-    own = gram[pl.ds(pl.multiple_of(z * (few * n_x), 8), few * n_x), :]
-    terms = three_terms(own)
-    for i in range(count):
-        at = i % n_x
-        pack[i, 0:piece, :] = flat[i * piece : (i + 1) * piece, :]
-        for j, term in enumerate(terms):
-            pack[i, piece + j * few : piece + (j + 1) * few, :] = term[at * few : (at + 1) * few]
-    o_ref[...] = pack[...].astype(BF16)
-
-
-def packets_of(place, hidden, grad_out, error, p_sum, n_x, n_z, n_tensor):
+    block = width // n_tensor
+    blocks = n_tensor // 2
+    for target, owner in ((send_ref, 1 - core), (keep_ref, core)):
+        for i in range(blocks):
+            start = pl.multiple_of((2 * i + owner) * block, 8)
+            target[i * block : (i + 1) * block, :] = flat[pl.ds(start, block), :]
+        few = target.shape[0] - blocks * block
+        target[blocks * block :, :] = gram[pl.ds(pl.multiple_of(z * few, 8), few), :]
+
+
+def right_terms(hidden, grad_out, error, p_sum, n_x, n_z, n_tensor):
     tokens, rows = hidden.shape
     width = grad_out.shape[1]
     half = error.shape[2]
     rank = p_sum.shape[1]
-    cuts = 4
-    count = n_tensor * n_x
-    deep = width // count + 3 * (rank // (n_x * n_z))
-    return call(
-        functools.partial(packet_kernel, n_x, n_z, cuts),
-        jax.ShapeDtypeStruct((count, deep, rank), BF16),
+    kept = jax.ShapeDtypeStruct((width // 2 + rank // n_z, rank), F32)
+    return call(
+        functools.partial(right_term_kernel, n_x, n_tensor),
+        (kept, kept),
         [
-            pltpu.VMEM((tokens, rows), BF16),
-            pltpu.VMEM((tokens, width), BF16),
-            pltpu.VMEM((rows, half), BF16),
             pltpu.VMEM((rank, width), F32),
             pltpu.VMEM((width, rank), F32),
-            pltpu.VMEM((count, deep, rank), F32),
             pltpu.VMEM((rank, rank), F32),
-            pltpu.SemaphoreType.DMA((2 + cuts,)),
         ],
         2 * rank * (tokens * (width + rows) + rows * half),
         2 * (tokens * (width + rows) + rows * half + rows * rank),
-        [IN_SMEM, ANYWHERE, ANYWHERE, ANYWHERE, IN_VMEM],
-    )(place, hidden, grad_out, error, p_sum)
+        [IN_VMEM] * 4,
+    )(hidden, grad_out, error, p_sum)
+
+
+def pack_kernel(n_x, piece, few, keep_ref, came_ref, o_ref, total, pack):
+    total[...] = keep_ref[...] + came_ref[...]
+    count = o_ref.shape[0]
+    terms = three_terms(total[count * piece :, :])
+    for i in range(count):
+        at = i % n_x
+        pack[i, 0:piece, :] = total[i * piece : (i + 1) * piece, :]
+        for j, term in enumerate(terms):
+            pack[i, piece + j * few : piece + (j + 1) * few, :] = term[at * few : (at + 1) * few]
+    o_ref[...] = pack[...].astype(BF16)
+
+
+def packets_of(kept, came, n_x, count, few):
+    rows, rank = kept.shape
+    piece = (rows - n_x * few) // count
+    deep = piece + 3 * few
+    return call(
+        functools.partial(pack_kernel, n_x, piece, few),
+        jax.ShapeDtypeStruct((count, deep, rank), BF16),
+        [pltpu.VMEM((rows, rank), F32), pltpu.VMEM((count, deep, rank), F32)],
+        rows * rank,
+        8 * rows * rank + 2 * count * deep * rank,
+        [IN_VMEM, IN_VMEM],
+    )(kept, came)
 
 
 def repack_kernel(few, in_ref, o_ref, pack):
@@ -359,17 +378,19 @@
     n_x, n_z = lax.axis_size("x"), lax.axis_size("z")
     n_dp, n_tensor = lax.axis_size(DP), lax.axis_size(TENSOR)
     replicas = n_dp // 2
-    place = jnp.stack([lax.axis_index("x"), lax.axis_index("z")]).astype(jnp.int32)
     rows, rank = hidden.shape[1], q_init.shape[1]
     few = rank // n_dp
     chunk = round_up(-(-rows // n_dp), 8)
 
     q_whole = lax.all_gather(q_init, TENSOR, axis=0, tiled=True)
-    pieces = left_term(place, hidden, grad_out, error, q_whole, n_dp, chunk)
+    tokens, q_own = token_term(hidden, grad_out, q_whole, error.shape[2])
+    pieces = left_term(error, q_own, tokens, n_dp, chunk)
     pieces = mean_of_blocks(swap_blocks(pieces, DP), 1.0 / replicas)
     p_sum = swap_blocks(pieces, DP).reshape(n_dp * chunk, rank)
-    packets = packets_of(place, hidden, grad_out, error, p_sum, n_x, n_z, n_tensor)
-    packets = repacked(swap_blocks(packets, TENSOR + ("x",)), few, n_dp)
+    sent, kept = right_terms(hidden, grad_out, error, p_sum, n_x, n_z, n_tensor)
+    came = lax.ppermute(sent, "core", [(0, 1), (1, 0)])
+    packets = packets_of(kept, came, n_x, n_x * (n_tensor // 2), few)
+    packets = repacked(swap_blocks(packets, ("y", "x")), few, n_dp)
     return finished(swap_blocks(packets, DP), p_sum, rows, n_x, n_z, few)
 
 

time: 137 us -> 124 us (0.905)
  blocking collectives: 93.1 us -> 86.3 us
  Pallas kernels: 17.8 us -> 13.4 us
  local copies, waits for them, and re-layouts: 4.1 us -> 0.02 us
  waiting for transfers between devices: 14.2 us -> 15.7 us
    all_to_all x3, blocking collectives: 73.7 us -> 65.3 us  [swap_blocks(): return lax.all_to_all(blocks, axis, 0, 0, tiled=True)]
    pallas_call x2 -> x4, Pallas kernels: 9.32 us -> 4.97 us  [the longest x1 2.35 us: token_term(): call(token_term_kernel, (jax.ShapeDtypeStruct((rows, rank), F32), jax.Sha...]
    unnamed x10 -> x6, local copies, waits for them, and re-layouts: 4.1 us -> 0.02 us
    ppermute x0 -> x1, waiting for transfers between devices: none -> 1.98 us  [shards(): came = lax.ppermute(sent, 'core', [(0, 1), (1, 0)])]
    ppermute x0 -> x1, starting transfers between devices: none -> 1.92 us  [shards(): came = lax.ppermute(sent, 'core', [(0, 1), (1, 0)])]
    all_gather x1, blocking collectives: 19.4 us -> 21 us  [shards(): q_whole = lax.all_gather(q_init, TENSOR, axis=0, tiled=True)]
  transfers between devices with their start and end apart: 1 -> 2, of which waited for: 1 -> 2; matrix products, arithmetic and copies ran while one was open for 0% -> 0% of each run, Pallas kernels for 0% -> 0%
where the time goes in v3:
time: 124 us
  blocking collectives  86.3 us (70%)
  waiting for transfers between devices  15.7 us (13%)
  Pallas kernels  13.4 us (11%)
  starting transfers between devices  7.29 us (6%)
    all_to_all x3, blocking collectives, swap_blocks(): return lax.all_to_all(blocks, axis, 0, 0, tiled=True)  65.3 us
    all_gather x1, blocking collectives, shards(): q_whole = lax.all_gather(q_init, TENSOR, axis=0, tiled=True)  21 us
    all_to_all x1, waiting for transfers between devices, swap_blocks(): return lax.all_to_all(blocks, axis, 0, 0, tiled=True)  13.7 us
    pallas_call x1, Pallas kernels, finished(): call(functools.partial(finish_kernel, 2.0 / count), (jax.ShapeDtypeStruct...  7.56 us
    all_to_all x1, starting transfers between devices, swap_blocks(): return lax.all_to_all(blocks, axis, 0, 0, tiled=True)  5.37 us
  transfers between devices with their start and end apart: 2, of which 2 were waited for; matrix products, arithmetic and copies ran while one was open for 0% of the time, Pallas kernels for 0%

profile of v3, /device:TPU:64, one launch (start us, length us, event | category | flops | bytes accessed | tf_op | source)
XLA Modules:
  0.0 123.6 jit_solution(247535519177883859)
XLA Ops:
  0.6 0.0 copy-start
  0.6 21.0 %all_gather.3.q_hbm = bf16[2304,128]{1,0:T(8,128)(2,1)} all-gather(bf16[144,128]{1,0:T(8,128)(2,1)} %param.6), channel_id=1, replica_groups=mesh['x'=4,'z'=8,'y'=8,'core'=2] {'y','core'}, dimensions={0}, use_global_device_ids=true | all-gather | bytes 626688 | tf_op jit(solution)/shard_map/all_gather | solution.py:385
  21.6 2.3 %shard_map.59 = (f32[1152,128]{1,0:T(8,128)S(1)}, bf16[1152,128]{1,0:T(8,128)(2,1)S(1)}) custom-call(bf16[256,1152]{1,0:T(8,128)(2,1)} %hid_ref.1, bf16[256,2304]{1,0:T(8,128)(2,1)} %out_ref.1, bf16[2304,128]{1,0:T(8,128)(2,1)} %all_gather.3.q_hbm), custom_call_target="tpu_custom_call" | custom-call | flops 301989888 | bytes 2359296 | tf_op jit(solution)/shard_map/pallas_call | solution.py:95
  24.0 0.0 copy-done
  24.0 0.9 shard_map.60
  24.8 0.0 copy-start.1
  24.9 0.0 copy-start.2
  24.9 26.6 %all_to_all.20.in_ref = bf16[32,40,128]{2,1,0:T(8,128)(2,1)S(1)} all-to-all(bf16[32,40,128]{2,1,0:T(8,128)(2,1)S(1)} %shard_map.60), channel_id=1, replica_groups=mesh['x'=4,'z'=8,'y'=8,'core'=2] {'x','z'}, dimensions={0} | all-to-all | bytes 655360 | tf_op jit(solution)/shard_map/all_to_all | solution.py:21
  51.5 0.1 shard_map.61
  51.6 17.8 %all_to_all.21 = bf16[32,40,128]{2,1,0:T(8,128)(2,1)S(1)} all-to-all(bf16[32,40,128]{2,1,0:T(8,128)(2,1)S(1)} %shard_map.61), channel_id=1, replica_groups=mesh['x'=4,'z'=8,'y'=8,'core'=2] {'x','z'}, dimensions={0} | all-to-all | bytes 655360 | tf_op jit(solution)/shard_map/all_to_all | solution.py:21
  69.4 0.0 copy-done.1
  69.4 0.0 copy-done.2
  69.4 1.7 %shard_map.62 = (f32[1168,128]{1,0:T(8,128)S(1)}, f32[1168,128]{1,0:T(8,128)S(1)}) custom-call(bf16[256,1152]{1,0:T(8,128)(2,1)S(1)} %copy-done.2, bf16[256,2304]{1,0:T(8,128)(2,1)S(1)} %copy-done.1, bf16[1,1152,1152]{2,1,0:T(8,128)(2,1)S(1)} %copy-done, bf16[1280,128]{1,0:T(8,128)(2,1)S(1)} %bitcast.2), custom_call_target="tpu_custom_call" | custom-call | flops 566231040 | bytes 4718592 | tf_op jit(solution)/shard_map/pallas_call | solution.py:198
  71.0 1.9 %collective-permute-start = (f32[1168,128]{1,0:T(8,128)S(1)}, f32[1168,128]{1,0:T(8,128)S(1)}, u32[]{:S(2)}, u32[]{:S(2)}) collective-permute-start(f32[1168,128]{1,0:T(8,128)S(1)} %get-tuple-element.9), channel_id=1, source_target_pairs={{0,1},{1,0},{2,3},{3,2},{4,5},{5,4},{6,7},{7,6},{8,9},{9,8},{10,11... | collective-permute-start | bytes 1794056 | tf_op jit(solution)/shard_map/ppermute | solution.py:391
  73.0 2.0 %collective-permute-done.came_ref = f32[1168,128]{1,0:T(8,128)S(1)} collective-permute-done((f32[1168,128]{1,0:T(8,128)S(1)}, f32[1168,128]{1,0:T(8,128)S(1)}, u32[]{:S(2)}, u32[]{:S(2)}) %collective-permute-start) | collective-permute-done | bytes 598048 | tf_op jit(solution)/shard_map/ppermute | solution.py:391
  75.0 0.1 shard_map.63
  75.1 20.8 %all_to_all.22.in_ref = bf16[32,48,128]{2,1,0:T(8,128)(2,1)S(1)} all-to-all(bf16[32,48,128]{2,1,0:T(8,128)(2,1)S(1)} %shard_map.63), channel_id=1, replica_groups=mesh['x'=4,'z'=8,'y'=8,'core'=2] {'y','x'}, dimensions={0} | all-to-all | bytes 786432 | tf_op jit(solution)/shard_map/all_to_all | solution.py:21
  95.9 0.8 shard_map.64
  96.7 5.4 %all-to-all-start.3 = ((bf16[32,48,128]{2,1,0:T(8,128)(2,1)}), bf16[32,48,128]{2,1,0:T(8,128)(2,1)S(1)}, u32[]{:S(2)}, u32[]{:S(2)}) async-start(bf16[32,48,128]{2,1,0:T(8,128)(2,1)} %shard_map.64), calls=%async_computation.3 | async-start | bytes 786432 | tf_op jit(solution)/shard_map/all_to_all | solution.py:21
  102.2 0.2 fusion.pick_ref
  102.3 13.7 %all-to-all-done.3 = bf16[32,48,128]{2,1,0:T(8,128)(2,1)S(1)} async-done(((bf16[32,48,128]{2,1,0:T(8,128)(2,1)}), bf16[32,48,128]{2,1,0:T(8,128)(2,1)S(1)}, u32[]{:S(2)}, u32[]{:S(2)}) %all-to-all-start.3) | async-done | bytes 393248 | tf_op jit(solution)/shard_map/all_to_all | solution.py:21
  116.0 7.6 %shard_map.65 = (bf16[1152,128]{1,0:T(8,128)(2,1)}, bf16[144,128]{1,0:T(8,128)(2,1)}) custom-call(bf16[272,1536]{1,0:T(8,128)(2,1)S(1)} %fusion.pick_ref, bf16[1536,128]{1,0:T(8,128)(2,1)S(1)} %bitcast.4, bf16[1280,128]{1,0:T(8,128)(2,1)S(1)} %bitcast.3), custom_call_target="tpu_custom_call" | custom-call | flops 220200960 | bytes 1425408 | tf_op jit(solution)/shard_map/pallas_call | solution.py:364
  (1 shorter events, 0.0 us)
Async XLA Ops:
  0.6 23.3 %copy-start = (bf16[1,1152,1152]{2,1,0:T(8,128)(2,1)S(1)}, bf16[1,1152,1152]{2,1,0:T(8,128)(2,1)}, u32[]{:S(2)}) copy-start(bf16[1,1152,1152]{2,1,0:T(8,128)(2,1)} %err_ref.3) | copy-start | bytes 7962628
  24.8 44.5 %copy-start.1 = (bf16[256,2304]{1,0:T(8,128)(2,1)S(1)}, bf16[256,2304]{1,0:T(8,128)(2,1)}, u32[]{:S(2)}) copy-start(bf16[256,2304]{1,0:T(8,128)(2,1)} %out_ref.1) | copy-start | bytes 3538948
  24.9 44.5 %copy-start.2 = (bf16[256,1152]{1,0:T(8,128)(2,1)S(1)}, bf16[256,1152]{1,0:T(8,128)(2,1)}, u32[]{:S(2)}) copy-start(bf16[256,1152]{1,0:T(8,128)(2,1)} %hid_ref.1) | copy-start | bytes 1769476
  71.0 3.9 %collective-permute-start = (f32[1168,128]{1,0:T(8,128)S(1)}, f32[1168,128]{1,0:T(8,128)S(1)}, u32[]{:S(2)}, u32[]{:S(2)}) collective-permute-start(f32[1168,128]{1,0:T(8,128)S(1)} %get-tuple-element.9), channel_id=1, source_target_pairs={{0,1},{1,0},{2,3},{3,2},{4,5},{5,4},{6,7},{7,6},{8,9},{9,8},{10,11... | collective-permute-start | bytes 1794056 | tf_op jit(solution)/shard_map/ppermute | solution.py:391
  96.7 19.3 %all-to-all-start.3 = ((bf16[32,48,128]{2,1,0:T(8,128)(2,1)}), bf16[32,48,128]{2,1,0:T(8,128)(2,1)S(1)}, u32[]{:S(2)}, u32[]{:S(2)}) async-start(bf16[32,48,128]{2,1,0:T(8,128)(2,1)} %shard_map.64), calls=%async_computation.3 | async-start | bytes 786432 | tf_op jit(solution)/shard_map/all_to_all | solution.py:21

commit v4 on v3

--- a/solution.py
+++ b/solution.py
@@ -2,6 +2,8 @@
 
 import jax
 import jax.numpy as jnp
+import ml_dtypes
+import numpy as np
 from jax import lax
 from jax.experimental import pallas as pl
 from jax.experimental.pallas import tpu as pltpu
@@ -12,6 +14,7 @@
 BF16 = jnp.bfloat16
 DP = ("x", "z")
 TENSOR = ("y", "core")
+ROUND = ("z", "x")
 VMEM_BYTES = 32 * 2**20
 VMEM_MOST = 53 * 2**20
 STEP = 8
@@ -270,9 +273,7 @@
             a[i, j] = jnp.broadcast_to(block[i : i + 1, j : j + 1], like)
     inverse = {}
     for j in range(size):
-        pivot = a[j, j]
-        scale = lax.rsqrt(pivot)
-        scale = scale * (1.5 - (0.5 * pivot) * (scale * scale))
+        scale = lax.rsqrt(a[j, j])
         for m in range(j):
             inverse[j, m] = inverse[j, m] * scale
         inverse[j, j] = scale
@@ -327,9 +328,8 @@
 
 def finish_kernel(scale, pick_ref, in_ref, p_ref, p_out, q_out):
     rank = p_ref.shape[1]
-    summed = dot(pick_ref[...], in_ref[...])
-    inverse = inverse_factor(summed[:rank])
-    s_sum = summed[rank:] * scale
+    inverse = inverse_factor(dot(pick_ref[:rank, :], in_ref[...]))
+    s_sum = dot(pick_ref[rank:, :], in_ref[...]) * scale
     terms = [term.astype(BF16) for term in three_terms(inverse)]
     p_low = p_ref[: p_out.shape[0], :]
     p_new = dot_cols(p_low, terms[2]) + dot_cols(p_low, terms[1])
@@ -346,21 +346,17 @@
 
 def pick_rows(n_x, n_z, piece, few, rank):
     deep = piece + 3 * few
-    count = n_x * n_z
-    source = lax.broadcasted_iota(jnp.int32, (1, count * deep), 1)
+    source = np.arange(n_x * n_z * deep)
     device, row = source // deep, source % deep
-    x, z = device // n_z, device % n_z
-    gram_row = z * (few * n_x) + x * few + (row - piece) % few
-    factor_row = rank + x * piece + row
-    target = jnp.where(row < piece, factor_row, gram_row)
-    rows = lax.broadcasted_iota(jnp.int32, (rank + n_x * piece, 1), 0)
-    return (rows == target).astype(BF16)
-
-
-def finished(packets, p_sum, rows, n_x, n_z, few):
+    z, x = device // n_x, device % n_x
+    gram_row = (z * n_x + x) * few + (row - piece) % few
+    target = np.where(row < piece, rank + x * piece + row, gram_row)
+    return (np.arange(rank + n_x * piece)[:, None] == target[None, :]).astype(ml_dtypes.bfloat16)
+
+
+def finished(pick, packets, p_sum, rows, n_x, few):
     count, deep, rank = packets.shape
     piece = deep - 3 * few
-    pick = pick_rows(n_x, n_z, piece, few, rank)
     return call(
         functools.partial(finish_kernel, 2.0 / count),
         (
@@ -385,13 +381,14 @@
     q_whole = lax.all_gather(q_init, TENSOR, axis=0, tiled=True)
     tokens, q_own = token_term(hidden, grad_out, q_whole, error.shape[2])
     pieces = left_term(error, q_own, tokens, n_dp, chunk)
-    pieces = mean_of_blocks(swap_blocks(pieces, DP), 1.0 / replicas)
-    p_sum = swap_blocks(pieces, DP).reshape(n_dp * chunk, rank)
+    pieces = mean_of_blocks(swap_blocks(pieces, ROUND), 1.0 / replicas)
+    p_sum = swap_blocks(pieces, ROUND).reshape(n_dp * chunk, rank)
     sent, kept = right_terms(hidden, grad_out, error, p_sum, n_x, n_z, n_tensor)
     came = lax.ppermute(sent, "core", [(0, 1), (1, 0)])
     packets = packets_of(kept, came, n_x, n_x * (n_tensor // 2), few)
     packets = repacked(swap_blocks(packets, ("y", "x")), few, n_dp)
-    return finished(swap_blocks(packets, DP), p_sum, rows, n_x, n_z, few)
+    pick = pick_rows(n_x, n_z, packets.shape[1] - 3 * few, few, rank)
+    return finished(jnp.asarray(pick), swap_blocks(packets, ROUND), p_sum, rows, n_x, few)
 
 
 def solution(mesh):

time: 124 us -> 121 us (0.976)
  the two profiles are of different devices: /device:TPU:64 before, /device:TPU:1 now
where the time goes in v4:
time: 121 us; the launch traced here: 120 us
  blocking collectives  100 us (83%)
  Pallas kernels  11.8 us (10%)
  starting transfers between devices  5.69 us (5%)
  waiting for transfers between devices  1.62 us (1%)
    all_to_all x4, blocking collectives, swap_blocks(): return lax.all_to_all(blocks, axis, 0, 0, tiled=True)  75.6 us
    all_gather x1, blocking collectives, shards(): q_whole = lax.all_gather(q_init, TENSOR, axis=0, tiled=True)  24.4 us
    pallas_call x1, Pallas kernels, finished(): call(functools.partial(finish_kernel, 2.0 / count), (jax.ShapeDtypeStruct...  6.6 us
    ppermute x1, starting transfers between devices, shards(): came = lax.ppermute(sent, 'core', [(0, 1), (1, 0)])  5.69 us
  transfers between devices with their start and end apart: 1, of which 1 were waited for; matrix products, arithmetic and copies ran while one was open for 0% of the time, Pallas kernels for 0%

profile of v4, /device:TPU:1, one launch (start us, length us, event | category | flops | bytes accessed | tf_op | source)
XLA Modules:
  0.0 119.8 jit_solution(7798821871623885565)
XLA Ops:
  0.6 0.0 copy-start
  0.6 24.4 %all_gather.3.q_hbm = bf16[2304,128]{1,0:T(8,128)(2,1)} all-gather(bf16[144,128]{1,0:T(8,128)(2,1)} %param.7), channel_id=1, replica_groups=mesh['x'=4,'z'=8,'y'=8,'core'=2] {'y','core'}, dimensions={0}, use_global_device_ids=true | all-gather | bytes 626688 | tf_op jit(solution)/shard_map/all_gather | solution.py:381
  25.1 2.4 %shard_map.68 = (f32[1152,128]{1,0:T(8,128)S(1)}, bf16[1152,128]{1,0:T(8,128)(2,1)S(1)}) custom-call(bf16[256,1152]{1,0:T(8,128)(2,1)} %hid_ref.1, bf16[256,2304]{1,0:T(8,128)(2,1)} %out_ref.1, bf16[2304,128]{1,0:T(8,128)(2,1)} %all_gather.3.q_hbm), custom_call_target="tpu_custom_call" | custom-call | flops 301989888 | bytes 2359296 | tf_op jit(solution)/shard_map/pallas_call | solution.py:98
  27.4 0.0 copy-done
  27.5 0.0 copy-start.1
  27.5 0.0 copy-start.2
  27.5 0.9 shard_map.69
  28.3 23.5 %all_to_all.20.in_ref = bf16[32,40,128]{2,1,0:T(8,128)(2,1)S(1)} all-to-all(bf16[32,40,128]{2,1,0:T(8,128)(2,1)S(1)} %shard_map.69), channel_id=1, replica_groups=mesh['x'=4,'z'=8,'y'=8,'core'=2] {'z','x'}, dimensions={0} | all-to-all | bytes 655360 | tf_op jit(solution)/shard_map/all_to_all | solution.py:24
  51.9 0.1 shard_map.70
  51.9 15.6 %all_to_all.21 = bf16[32,40,128]{2,1,0:T(8,128)(2,1)S(1)} all-to-all(bf16[32,40,128]{2,1,0:T(8,128)(2,1)S(1)} %shard_map.70), channel_id=1, replica_groups=mesh['x'=4,'z'=8,'y'=8,'core'=2] {'z','x'}, dimensions={0} | all-to-all | bytes 655360 | tf_op jit(solution)/shard_map/all_to_all | solution.py:24
  67.5 0.0 copy-done.1
  67.5 0.0 copy-done.2
  67.5 1.7 %shard_map.71 = (f32[1168,128]{1,0:T(8,128)S(1)}, f32[1168,128]{1,0:T(8,128)S(1)}) custom-call(bf16[256,1152]{1,0:T(8,128)(2,1)S(1)} %copy-done.2, bf16[256,2304]{1,0:T(8,128)(2,1)S(1)} %copy-done.1, bf16[1,1152,1152]{2,1,0:T(8,128)(2,1)S(1)} %copy-done, bf16[1280,128]{1,0:T(8,128)(2,1)S(1)} %bitcast.2), custom_call_target="tpu_custom_call" | custom-call | flops 566231040 | bytes 4718592 | tf_op jit(solution)/shard_map/pallas_call | solution.py:201
  69.2 0.0 copy-start.3
  69.2 5.7 %collective-permute-start = (f32[1168,128]{1,0:T(8,128)S(1)}, f32[1168,128]{1,0:T(8,128)S(1)}, u32[]{:S(2)}, u32[]{:S(2)}) collective-permute-start(f32[1168,128]{1,0:T(8,128)S(1)} %get-tuple-element.9), channel_id=1, source_target_pairs={{0,1},{1,0},{2,3},{3,2},{4,5},{5,4},{6,7},{7,6},{8,9},{9,8},{10,11... | collective-permute-start | bytes 1794056 | tf_op jit(solution)/shard_map/ppermute | solution.py:387
  74.9 1.6 %collective-permute-done.came_ref = f32[1168,128]{1,0:T(8,128)S(1)} collective-permute-done((f32[1168,128]{1,0:T(8,128)S(1)}, f32[1168,128]{1,0:T(8,128)S(1)}, u32[]{:S(2)}, u32[]{:S(2)}) %collective-permute-start) | collective-permute-done | bytes 598048 | tf_op jit(solution)/shard_map/ppermute | solution.py:387
  76.5 0.1 shard_map.72
  76.6 19.5 %all_to_all.22.in_ref = bf16[32,48,128]{2,1,0:T(8,128)(2,1)S(1)} all-to-all(bf16[32,48,128]{2,1,0:T(8,128)(2,1)S(1)} %shard_map.72), channel_id=1, replica_groups=mesh['x'=4,'z'=8,'y'=8,'core'=2] {'y','x'}, dimensions={0} | all-to-all | bytes 786432 | tf_op jit(solution)/shard_map/all_to_all | solution.py:24
  96.1 0.1 shard_map.73
  96.2 17.0 %all_to_all.23 = bf16[32,48,128]{2,1,0:T(8,128)(2,1)S(1)} all-to-all(bf16[32,48,128]{2,1,0:T(8,128)(2,1)S(1)} %shard_map.73), channel_id=1, replica_groups=mesh['x'=4,'z'=8,'y'=8,'core'=2] {'z','x'}, dimensions={0} | all-to-all | bytes 786432 | tf_op jit(solution)/shard_map/all_to_all | solution.py:24
  113.2 0.0 copy-done.3
  113.2 6.6 %shard_map.74 = (bf16[1152,128]{1,0:T(8,128)(2,1)}, bf16[144,128]{1,0:T(8,128)(2,1)}) custom-call(bf16[272,1536]{1,0:T(8,128)(2,1)S(1)} %copy-done.3, bf16[1536,128]{1,0:T(8,128)(2,1)S(1)} %bitcast.4, bf16[1280,128]{1,0:T(8,128)(2,1)S(1)} %bitcast.3), custom_call_target="tpu_custom_call" | custom-call | flops 220200960 | bytes 1425408 | tf_op jit(solution)/shard_map/pallas_call | solution.py:360
Async XLA Ops:
  0.6 26.8 %copy-start = (bf16[1,1152,1152]{2,1,0:T(8,128)(2,1)S(1)}, bf16[1,1152,1152]{2,1,0:T(8,128)(2,1)}, u32[]{:S(2)}) copy-start(bf16[1,1152,1152]{2,1,0:T(8,128)(2,1)} %err_ref.3) | copy-start | bytes 7962628
  27.5 40.1 %copy-start.1 = (bf16[256,2304]{1,0:T(8,128)(2,1)S(1)}, bf16[256,2304]{1,0:T(8,128)(2,1)}, u32[]{:S(2)}) copy-start(bf16[256,2304]{1,0:T(8,128)(2,1)} %out_ref.1) | copy-start | bytes 3538948
  27.5 40.1 %copy-start.2 = (bf16[256,1152]{1,0:T(8,128)(2,1)S(1)}, bf16[256,1152]{1,0:T(8,128)(2,1)}, u32[]{:S(2)}) copy-start(bf16[256,1152]{1,0:T(8,128)(2,1)} %hid_ref.1) | copy-start | bytes 1769476
  69.2 44.0 %copy-start.3 = (bf16[272,1536]{1,0:T(8,128)(2,1)S(1)}, bf16[272,1536]{1,0:T(8,128)(2,1)}, u32[]{:S(2)}) copy-start(bf16[272,1536]{1,0:T(8,128)(2,1)} %constant.2.clone.pick_ref) | copy-start | bytes 2506756
  69.2 7.3 %collective-permute-start = (f32[1168,128]{1,0:T(8,128)S(1)}, f32[1168,128]{1,0:T(8,128)S(1)}, u32[]{:S(2)}, u32[]{:S(2)}) collective-permute-start(f32[1168,128]{1,0:T(8,128)S(1)} %get-tuple-element.9), channel_id=1, source_target_pairs={{0,1},{1,0},{2,3},{3,2},{4,5},{5,4},{6,7},{7,6},{8,9},{9,8},{10,11... | collective-permute-start | bytes 1794056 | tf_op jit(solution)/shard_map/ppermute | solution.py:387

commit v5 on v4

--- a/solution.py
+++ b/solution.py
@@ -265,12 +265,17 @@
     )(packets)
 
 
-def small_factor(block, like):
-    size = block.shape[0]
-    a = {}
-    for i in range(size):
-        for j in range(i + 1):
-            a[i, j] = jnp.broadcast_to(block[i : i + 1, j : j + 1], like)
+def across(tile, column):
+    return jnp.broadcast_to(tile[:, column : column + 1], tile.shape)
+
+
+def down(tile, row):
+    return jnp.broadcast_to(tile[row : row + 1, :], tile.shape)
+
+
+def small_factor(columns):
+    size = len(columns)
+    a = {(i, j): down(columns[j], i) for i in range(size) for j in range(i + 1)}
     inverse = {}
     for j in range(size):
         scale = lax.rsqrt(a[j, j])
@@ -287,41 +292,52 @@
     return inverse
 
 
+def weighted(inverse, items, row):
+    total = inverse[row, 0] * items[0]
+    for m in range(1, row + 1):
+        total = total + inverse[row, m] * items[m]
+    return total
+
+
 def inverse_factor(gram):
     rank = gram.shape[0]
-    like = (STEP, rank)
-    lane = lax.broadcasted_iota(jnp.int32, like, 1)
-    tiles = [gram[b * STEP : (b + 1) * STEP, :] for b in range(rank // STEP)]
+    count = rank // STEP
+    lane = lax.broadcasted_iota(jnp.int32, (STEP, rank), 1)
+    sublane = lax.broadcasted_iota(jnp.int32, (STEP, rank), 0)
+    tiles = [gram[b * STEP : (b + 1) * STEP, :] for b in range(count)]
+    block = [across(tiles[0], j) for j in range(STEP)]
     done = []
-    for k in range(rank // STEP):
+    for k in range(count):
         first = k * STEP
-        inverse = small_factor(tiles[k][:, first : first + STEP], like)
+        inverse = small_factor(block)
         inside = (lane >= first) & (lane < first + STEP)
         pivots = []
         for m in range(STEP):
-            row = jnp.broadcast_to(tiles[k][m : m + 1, :], like)
-            pivots.append(jnp.where(inside, jnp.where(lane == first + m, 1.0, 0.0), row))
-        scaled = []
-        for i in range(STEP):
-            row = inverse[i, 0] * pivots[0]
-            for m in range(1, i + 1):
-                row = row + inverse[i, m] * pivots[m]
-            scaled.append(row)
-        sublane = lax.broadcasted_iota(jnp.int32, like, 0)
+            unit = jnp.where(lane == first + m, 1.0, 0.0)
+            pivots.append(jnp.where(inside, unit, down(tiles[k], m)))
+        scaled = [weighted(inverse, pivots, i) for i in range(STEP)]
         rows = scaled[0]
         for i in range(1, STEP):
             rows = jnp.where(sublane == i, scaled[i], rows)
         done.append(jnp.where(lane <= first + sublane, rows, 0.0))
-        for b in range(k + 1, rank // STEP):
-            columns = [
-                jnp.broadcast_to(tiles[b][:, first + m : first + m + 1], like) for m in range(STEP)
-            ]
+        solved = []
+        for m in range(STEP):
+            row = inverse[m, m] * scaled[m]
+            for i in range(m + 1, STEP):
+                row = row + inverse[i, m] * scaled[i]
+            solved.append(row)
+        for b in range(k + 1, count):
+            columns = [across(tiles[b], first + m) for m in range(STEP)]
             tile = jnp.where(inside, 0.0, tiles[b])
-            for i in range(STEP):
-                factor = inverse[i, 0] * columns[0]
-                for m in range(1, i + 1):
-                    factor = factor + inverse[i, m] * columns[m]
-                tile = tile - factor * scaled[i]
+            if b == k + 1:
+                block = [across(tiles[b], first + STEP + j) for j in range(STEP)]
+                factors = [weighted(inverse, columns, i) for i in range(STEP)]
+                for i, factor in enumerate(factors):
+                    tile = tile - factor * scaled[i]
+                    block = [block[j] - factor * down(factor, j) for j in range(STEP)]
+            else:
+                for m in range(STEP):
+                    tile = tile - columns[m] * solved[m]
             tiles[b] = tile
     return jnp.concatenate(done, axis=0)
 

time: 121 us -> 120 us (level)
  Pallas kernels: 11.8 us -> 9.93 us
    pallas_call x1, Pallas kernels: 6.6 us -> 4.77 us  [finished(): call(functools.partial(finish_kernel, 2.0 / count), (jax.ShapeDtypeStruct...]
where the time goes in v5:
time: 120 us; the launch traced here: 118 us
  blocking collectives  100 us (83%)
  Pallas kernels  9.93 us (8%)
  starting transfers between devices  5.69 us (5%)
  waiting for transfers between devices  1.62 us (1%)
    all_to_all x4, blocking collectives, swap_blocks(): return lax.all_to_all(blocks, axis, 0, 0, tiled=True)  75.6 us
    all_gather x1, blocking collectives, shards(): q_whole = lax.all_gather(q_init, TENSOR, axis=0, tiled=True)  24.4 us
    ppermute x1, starting transfers between devices, shards(): came = lax.ppermute(sent, 'core', [(0, 1), (1, 0)])  5.69 us
    pallas_call x1, Pallas kernels, finished(): call(functools.partial(finish_kernel, 2.0 / count), (jax.ShapeDtypeStruct...  4.77 us
  transfers between devices with their start and end apart: 1, of which 1 were waited for; matrix products, arithmetic and copies ran while one was open for 0% of the time, Pallas kernels for 0%

profile of v5, /device:TPU:1, one launch (start us, length us, event | category | flops | bytes accessed | tf_op | source)
XLA Modules:
  0.0 118.0 jit_solution(1957259633573904166)
XLA Ops:
  0.6 0.0 copy-start
  0.6 24.4 %all_gather.3.q_hbm = bf16[2304,128]{1,0:T(8,128)(2,1)} all-gather(bf16[144,128]{1,0:T(8,128)(2,1)} %param.7), channel_id=1, replica_groups=mesh['x'=4,'z'=8,'y'=8,'core'=2] {'y','core'}, dimensions={0}, use_global_device_ids=true | all-gather | bytes 626688 | tf_op jit(solution)/shard_map/all_gather | solution.py:397
  25.1 2.4 %shard_map.68 = (f32[1152,128]{1,0:T(8,128)S(1)}, bf16[1152,128]{1,0:T(8,128)(2,1)S(1)}) custom-call(bf16[256,1152]{1,0:T(8,128)(2,1)} %hid_ref.1, bf16[256,2304]{1,0:T(8,128)(2,1)} %out_ref.1, bf16[2304,128]{1,0:T(8,128)(2,1)} %all_gather.3.q_hbm), custom_call_target="tpu_custom_call" | custom-call | flops 301989888 | bytes 2359296 | tf_op jit(solution)/shard_map/pallas_call | solution.py:98
  27.4 0.0 copy-done
  27.5 0.0 copy-start.1
  27.5 0.0 copy-start.2
  27.5 0.9 shard_map.69
  28.3 23.5 %all_to_all.20.in_ref = bf16[32,40,128]{2,1,0:T(8,128)(2,1)S(1)} all-to-all(bf16[32,40,128]{2,1,0:T(8,128)(2,1)S(1)} %shard_map.69), channel_id=1, replica_groups=mesh['x'=4,'z'=8,'y'=8,'core'=2] {'z','x'}, dimensions={0} | all-to-all | bytes 655360 | tf_op jit(solution)/shard_map/all_to_all | solution.py:24
  51.9 0.1 shard_map.70
  51.9 15.6 %all_to_all.21 = bf16[32,40,128]{2,1,0:T(8,128)(2,1)S(1)} all-to-all(bf16[32,40,128]{2,1,0:T(8,128)(2,1)S(1)} %shard_map.70), channel_id=1, replica_groups=mesh['x'=4,'z'=8,'y'=8,'core'=2] {'z','x'}, dimensions={0} | all-to-all | bytes 655360 | tf_op jit(solution)/shard_map/all_to_all | solution.py:24
  67.5 0.0 copy-done.1
  67.5 0.0 copy-done.2
  67.5 1.7 %shard_map.71 = (f32[1168,128]{1,0:T(8,128)S(1)}, f32[1168,128]{1,0:T(8,128)S(1)}) custom-call(bf16[256,1152]{1,0:T(8,128)(2,1)S(1)} %copy-done.2, bf16[256,2304]{1,0:T(8,128)(2,1)S(1)} %copy-done.1, bf16[1,1152,1152]{2,1,0:T(8,128)(2,1)S(1)} %copy-done, bf16[1280,128]{1,0:T(8,128)(2,1)S(1)} %bitcast.2), custom_call_target="tpu_custom_call" | custom-call | flops 566231040 | bytes 4718592 | tf_op jit(solution)/shard_map/pallas_call | solution.py:201
  69.2 0.0 copy-start.3
  69.2 5.7 %collective-permute-start = (f32[1168,128]{1,0:T(8,128)S(1)}, f32[1168,128]{1,0:T(8,128)S(1)}, u32[]{:S(2)}, u32[]{:S(2)}) collective-permute-start(f32[1168,128]{1,0:T(8,128)S(1)} %get-tuple-element.9), channel_id=1, source_target_pairs={{0,1},{1,0},{2,3},{3,2},{4,5},{5,4},{6,7},{7,6},{8,9},{9,8},{10,11... | collective-permute-start | bytes 1794056 | tf_op jit(solution)/shard_map/ppermute | solution.py:403
  74.9 1.6 %collective-permute-done.came_ref = f32[1168,128]{1,0:T(8,128)S(1)} collective-permute-done((f32[1168,128]{1,0:T(8,128)S(1)}, f32[1168,128]{1,0:T(8,128)S(1)}, u32[]{:S(2)}, u32[]{:S(2)}) %collective-permute-start) | collective-permute-done | bytes 598048 | tf_op jit(solution)/shard_map/ppermute | solution.py:403
  76.5 0.1 shard_map.72
  76.6 19.5 %all_to_all.22.in_ref = bf16[32,48,128]{2,1,0:T(8,128)(2,1)S(1)} all-to-all(bf16[32,48,128]{2,1,0:T(8,128)(2,1)S(1)} %shard_map.72), channel_id=1, replica_groups=mesh['x'=4,'z'=8,'y'=8,'core'=2] {'y','x'}, dimensions={0} | all-to-all | bytes 786432 | tf_op jit(solution)/shard_map/all_to_all | solution.py:24
  96.1 0.1 shard_map.73
  96.2 17.0 %all_to_all.23 = bf16[32,48,128]{2,1,0:T(8,128)(2,1)S(1)} all-to-all(bf16[32,48,128]{2,1,0:T(8,128)(2,1)S(1)} %shard_map.73), channel_id=1, replica_groups=mesh['x'=4,'z'=8,'y'=8,'core'=2] {'z','x'}, dimensions={0} | all-to-all | bytes 786432 | tf_op jit(solution)/shard_map/all_to_all | solution.py:24
  113.2 0.0 copy-done.3
  113.2 4.8 %shard_map.74 = (bf16[1152,128]{1,0:T(8,128)(2,1)}, bf16[144,128]{1,0:T(8,128)(2,1)}) custom-call(bf16[272,1536]{1,0:T(8,128)(2,1)S(1)} %copy-done.3, bf16[1536,128]{1,0:T(8,128)(2,1)S(1)} %bitcast.4, bf16[1280,128]{1,0:T(8,128)(2,1)S(1)} %bitcast.3), custom_call_target="tpu_custom_call" | custom-call | flops 220200960 | bytes 1425408 | tf_op jit(solution)/shard_map/pallas_call | solution.py:376
Async XLA Ops:
  0.6 26.8 %copy-start = (bf16[1,1152,1152]{2,1,0:T(8,128)(2,1)S(1)}, bf16[1,1152,1152]{2,1,0:T(8,128)(2,1)}, u32[]{:S(2)}) copy-start(bf16[1,1152,1152]{2,1,0:T(8,128)(2,1)} %err_ref.3) | copy-start | bytes 7962628
  27.5 40.1 %copy-start.1 = (bf16[256,2304]{1,0:T(8,128)(2,1)S(1)}, bf16[256,2304]{1,0:T(8,128)(2,1)}, u32[]{:S(2)}) copy-start(bf16[256,2304]{1,0:T(8,128)(2,1)} %out_ref.1) | copy-start | bytes 3538948
  27.5 40.1 %copy-start.2 = (bf16[256,1152]{1,0:T(8,128)(2,1)S(1)}, bf16[256,1152]{1,0:T(8,128)(2,1)}, u32[]{:S(2)}) copy-start(bf16[256,1152]{1,0:T(8,128)(2,1)} %hid_ref.1) | copy-start | bytes 1769476
  69.2 44.0 %copy-start.3 = (bf16[272,1536]{1,0:T(8,128)(2,1)S(1)}, bf16[272,1536]{1,0:T(8,128)(2,1)}, u32[]{:S(2)}) copy-start(bf16[272,1536]{1,0:T(8,128)(2,1)} %constant.2.clone.pick_ref) | copy-start | bytes 2506756
  69.2 7.3 %collective-permute-start = (f32[1168,128]{1,0:T(8,128)S(1)}, f32[1168,128]{1,0:T(8,128)S(1)}, u32[]{:S(2)}, u32[]{:S(2)}) collective-permute-start(f32[1168,128]{1,0:T(8,128)S(1)} %get-tuple-element.9), channel_id=1, source_target_pairs={{0,1},{1,0},{2,3},{3,2},{4,5},{5,4},{6,7},{7,6},{8,9},{9,8},{10,11... | collective-permute-start | bytes 1794056 | tf_op jit(solution)/shard_map/ppermute | solution.py:403

commit v6 on v5

--- a/solution.py
+++ b/solution.py
@@ -16,7 +16,7 @@
 TENSOR = ("y", "core")
 ROUND = ("z", "x")
 VMEM_BYTES = 32 * 2**20
-VMEM_MOST = 53 * 2**20
+VMEM_MOST = 51 * 2**20
 STEP = 8
 
 

time: 120 us -> 119 us (level)
  blocking collectives: 100 us -> 98.6 us
    all_gather x1, blocking collectives: 24.4 us -> 23.1 us  [shards(): q_whole = lax.all_gather(q_init, TENSOR, axis=0, tiled=True)]
where the time goes in v6:
time: 119 us; the launch traced here: 118 us
  blocking collectives  98.6 us (83%)
  Pallas kernels  9.86 us (8%)
  starting transfers between devices  5.69 us (5%)
  waiting for transfers between devices  1.62 us (1%)
    all_to_all x4, blocking collectives, swap_blocks(): return lax.all_to_all(blocks, axis, 0, 0, tiled=True)  75.5 us
    all_gather x1, blocking collectives, shards(): q_whole = lax.all_gather(q_init, TENSOR, axis=0, tiled=True)  23.1 us
    ppermute x1, starting transfers between devices, shards(): came = lax.ppermute(sent, 'core', [(0, 1), (1, 0)])  5.69 us
    pallas_call x1, Pallas kernels, finished(): call(functools.partial(finish_kernel, 2.0 / count), (jax.ShapeDtypeStruct...  4.78 us
  transfers between devices with their start and end apart: 1, of which 1 were waited for; matrix products, arithmetic and copies ran while one was open for 0% of the time, Pallas kernels for 0%

profile of v6, /device:TPU:1, one launch (start us, length us, event | category | flops | bytes accessed | tf_op | source)
XLA Modules:
  0.0 117.6 jit_solution(12383193340184621593)
XLA Ops:
  0.6 0.0 copy-start
  0.6 23.1 %all_gather.3.q_hbm = bf16[2304,128]{1,0:T(8,128)(2,1)S(1)} all-gather(bf16[144,128]{1,0:T(8,128)(2,1)} %param.7), channel_id=1, replica_groups=mesh['x'=4,'z'=8,'y'=8,'core'=2] {'y','core'}, dimensions={0}, use_global_device_ids=true | all-gather | bytes 626688 | tf_op jit(solution)/shard_map/all_gather | solution.py:397
  23.8 0.0 copy-start.2
  23.8 1.1 copy-done.2
  24.8 2.3 %shard_map.68 = (f32[1152,128]{1,0:T(8,128)S(1)}, bf16[1152,128]{1,0:T(8,128)(2,1)S(1)}) custom-call(bf16[256,1152]{1,0:T(8,128)(2,1)S(1)} %copy-done.2, bf16[256,2304]{1,0:T(8,128)(2,1)} %out_ref.1, bf16[2304,128]{1,0:T(8,128)(2,1)S(1)} %all_gather.3.q_hbm), custom_call_target="tpu_custom_call" | custom-call | flops 301989888 | bytes 2359296 | tf_op jit(solution)/shard_map/pallas_call | solution.py:98
  27.1 0.0 copy-done
  27.1 0.0 copy-start.1
  27.2 0.9 shard_map.69
  28.0 23.4 %all_to_all.20.in_ref = bf16[32,40,128]{2,1,0:T(8,128)(2,1)S(1)} all-to-all(bf16[32,40,128]{2,1,0:T(8,128)(2,1)S(1)} %shard_map.69), channel_id=1, replica_groups=mesh['x'=4,'z'=8,'y'=8,'core'=2] {'z','x'}, dimensions={0} | all-to-all | bytes 655360 | tf_op jit(solution)/shard_map/all_to_all | solution.py:24
  51.4 0.1 shard_map.70
  51.5 15.6 %all_to_all.21 = bf16[32,40,128]{2,1,0:T(8,128)(2,1)S(1)} all-to-all(bf16[32,40,128]{2,1,0:T(8,128)(2,1)S(1)} %shard_map.70), channel_id=1, replica_groups=mesh['x'=4,'z'=8,'y'=8,'core'=2] {'z','x'}, dimensions={0} | all-to-all | bytes 655360 | tf_op jit(solution)/shard_map/all_to_all | solution.py:24
  67.1 0.0 copy-done.1
  67.1 1.7 %shard_map.71 = (f32[1168,128]{1,0:T(8,128)S(1)}, f32[1168,128]{1,0:T(8,128)S(1)}) custom-call(bf16[256,1152]{1,0:T(8,128)(2,1)S(1)} %copy-done.2, bf16[256,2304]{1,0:T(8,128)(2,1)S(1)} %copy-done.1, bf16[1,1152,1152]{2,1,0:T(8,128)(2,1)S(1)} %copy-done, bf16[1280,128]{1,0:T(8,128)(2,1)S(1)} %bitcast.2), custom_call_target="tpu_custom_call" | custom-call | flops 566231040 | bytes 4718592 | tf_op jit(solution)/shard_map/pallas_call | solution.py:201
  68.8 0.0 copy-start.3
  68.8 5.7 %collective-permute-start = (f32[1168,128]{1,0:T(8,128)S(1)}, f32[1168,128]{1,0:T(8,128)S(1)}, u32[]{:S(2)}, u32[]{:S(2)}) collective-permute-start(f32[1168,128]{1,0:T(8,128)S(1)} %get-tuple-element.9), channel_id=1, source_target_pairs={{0,1},{1,0},{2,3},{3,2},{4,5},{5,4},{6,7},{7,6},{8,9},{9,8},{10,11... | collective-permute-start | bytes 1794056 | tf_op jit(solution)/shard_map/ppermute | solution.py:403
  74.5 1.6 %collective-permute-done.came_ref = f32[1168,128]{1,0:T(8,128)S(1)} collective-permute-done((f32[1168,128]{1,0:T(8,128)S(1)}, f32[1168,128]{1,0:T(8,128)S(1)}, u32[]{:S(2)}, u32[]{:S(2)}) %collective-permute-start) | collective-permute-done | bytes 598048 | tf_op jit(solution)/shard_map/ppermute | solution.py:403
  76.1 0.1 shard_map.72
  76.2 19.5 %all_to_all.22.in_ref = bf16[32,48,128]{2,1,0:T(8,128)(2,1)S(1)} all-to-all(bf16[32,48,128]{2,1,0:T(8,128)(2,1)S(1)} %shard_map.72), channel_id=1, replica_groups=mesh['x'=4,'z'=8,'y'=8,'core'=2] {'y','x'}, dimensions={0} | all-to-all | bytes 786432 | tf_op jit(solution)/shard_map/all_to_all | solution.py:24
  95.7 0.1 shard_map.73
  95.8 17.0 %all_to_all.23 = bf16[32,48,128]{2,1,0:T(8,128)(2,1)S(1)} all-to-all(bf16[32,48,128]{2,1,0:T(8,128)(2,1)S(1)} %shard_map.73), channel_id=1, replica_groups=mesh['x'=4,'z'=8,'y'=8,'core'=2] {'z','x'}, dimensions={0} | all-to-all | bytes 786432 | tf_op jit(solution)/shard_map/all_to_all | solution.py:24
  112.8 0.0 copy-done.3
  112.8 4.8 %shard_map.74 = (bf16[1152,128]{1,0:T(8,128)(2,1)}, bf16[144,128]{1,0:T(8,128)(2,1)}) custom-call(bf16[272,1536]{1,0:T(8,128)(2,1)S(1)} %copy-done.3, bf16[1536,128]{1,0:T(8,128)(2,1)S(1)} %bitcast.4, bf16[1280,128]{1,0:T(8,128)(2,1)S(1)} %bitcast.3), custom_call_target="tpu_custom_call" | custom-call | flops 220200960 | bytes 1425408 | tf_op jit(solution)/shard_map/pallas_call | solution.py:376
Async XLA Ops:
  0.6 26.5 %copy-start = (bf16[1,1152,1152]{2,1,0:T(8,128)(2,1)S(1)}, bf16[1,1152,1152]{2,1,0:T(8,128)(2,1)}, u32[]{:S(2)}) copy-start(bf16[1,1152,1152]{2,1,0:T(8,128)(2,1)} %err_ref.3) | copy-start | bytes 7962628
  23.8 1.1 copy-start.2
  27.1 40.0 %copy-start.1 = (bf16[256,2304]{1,0:T(8,128)(2,1)S(1)}, bf16[256,2304]{1,0:T(8,128)(2,1)}, u32[]{:S(2)}) copy-start(bf16[256,2304]{1,0:T(8,128)(2,1)} %out_ref.1) | copy-start | bytes 3538948
  68.8 44.0 %copy-start.3 = (bf16[272,1536]{1,0:T(8,128)(2,1)S(1)}, bf16[272,1536]{1,0:T(8,128)(2,1)}, u32[]{:S(2)}) copy-start(bf16[272,1536]{1,0:T(8,128)(2,1)} %constant.2.clone.pick_ref) | copy-start | bytes 2506756
  68.8 7.3 %collective-permute-start = (f32[1168,128]{1,0:T(8,128)S(1)}, f32[1168,128]{1,0:T(8,128)S(1)}, u32[]{:S(2)}, u32[]{:S(2)}) collective-permute-start(f32[1168,128]{1,0:T(8,128)S(1)} %get-tuple-element.9), channel_id=1, source_target_pairs={{0,1},{1,0},{2,3},{3,2},{4,5},{5,4},{6,7},{7,6},{8,9},{9,8},{10,11... | collective-permute-start | bytes 1794056 | tf_op jit(solution)/shard_map/ppermute | solution.py:403
